TPU v7x, 512 devices: a whole 4x4x16 slice. The times are simulated.
512 devices in a mesh: section: 16 (over z), dp: 32 (over x, y, core).
Axes of the slice: x: 4, y: 4, z: 16, core: 2. Of those that a mesh axis runs over, the one named last changes fastest.
Arguments:
- saved_inputs: bfloat16 [16, 2, 2048, 4096], P('section', None, 'dp'), may hold values from -6 to 6
- loss_grad: bfloat16 [2, 2048, 4096], P(None, 'dp'), may hold values from -6 to 6
- w_in: bfloat16 [16, 4096, 128], P('section'), may hold values from -0.09375 to 0.09375
- w_out: bfloat16 [16, 128, 4096], P('section'), may hold values from -0.5 to 0.5
- left_root: bfloat16 [16, 32, 4, 128, 128], P('section', 'dp'), as said below
- right_root: bfloat16 [16, 32, 4, 128, 128], P('section', 'dp'), as said below
- momentum: float32 [16, 32, 4, 128, 128], P('section', 'dp'), may hold values from -6 to 6
- owned_blocks: int32 [16, 32, 4], P('section'), may hold values from 0 to 63, as said below
- owned_count: int32 [16, 32], P('section'), may hold values from 0 to 4, as said below
Outputs:
- new_momentum: float32 [16, 32, 4, 128, 128], P('section', 'dp')
- search_in: bfloat16 [16, 4096, 128], P('section', 'dp')
- search_out: bfloat16 [16, 128, 4096], P('section', None, 'dp')
Inputs may be any that keep to these rules, and one draw needn't show every extreme that they name: `owned_blocks`: in each section every block id of 0 to 63 stands in exactly one owner's first owned_count slots; slots at or past the count hold 0. `owned_count`: sums to 64 over the owners of a section; some owner of every section holds 4 blocks. `left_root`: Symmetric. `right_root`: Symmetric.
All inputs are finite; a program needn't handle non-finite values.
Results may differ from a plain program's by a relative error of at most 0.035.
Values may be sent and summed in bfloat16 or wider, within the bound.
A program may use at most 64 MiB of HBM per device.

v0:
```python
import jax
import jax.numpy as jnp
from jax import lax
from jax.sharding import PartitionSpec as P

MOMENTUM_DECAY = 0.9


def passed_along(value, axis, steps):
    count = lax.axis_size(axis)
    initial, last = (max(0, -steps), min(count, count - steps))
    return lax.ppermute(value, axis, [(source, source + steps) for source in range(initial, last)])


def silu_slope(values):
    sigma = jax.nn.sigmoid(values)
    return sigma * (1.0 + values * (1.0 - sigma))


def contract_rows(left_side, right_side):
    return lax.dot_general(
        left_side, right_side, (((0,), (0,)), ((), ())), preferred_element_type=jnp.float32
    )


def contract_cols(left_side, right_side):
    return lax.dot_general(
        left_side, right_side, (((1,), (1,)), ((), ())), preferred_element_type=jnp.float32
    )


def on_device(
    saved_inputs, loss_grad, w_in, w_out, left_root, right_root, momentum, owned_blocks, owned_count
):
    section_count = lax.axis_size("section")
    section_index = lax.axis_index("section")
    micro = saved_inputs.shape[1]
    tokens = saved_inputs.shape[2]
    width = saved_inputs.shape[3]
    order = w_in.shape[2]
    owners = owned_blocks.shape[1]
    slots = owned_blocks.shape[2]
    row_blocks = width // order
    weight_in = w_in[0]
    weight_out = w_out[0]
    inputs_all = saved_inputs[0]

    def accumulate(pieces):
        totals, inputs, pre_grad, act, upper = pieces
        return (totals[0] + contract_rows(inputs, pre_grad), totals[1] + contract_rows(act, upper))

    def keep_totals(pieces):
        return pieces[0]

    def tick(step, carry):
        incoming, total_in, total_out = carry
        batch = step - (section_count - 1 - section_index)
        active = (batch >= 0) & (batch < micro)
        chosen = jnp.clip(batch, 0, micro - 1)
        inputs = lax.dynamic_index_in_dim(inputs_all, chosen, 0, keepdims=False)
        given = lax.dynamic_index_in_dim(loss_grad, chosen, 0, keepdims=False)
        upper = jnp.where(section_index == section_count - 1, given, incoming)
        pre = jnp.dot(inputs, weight_in, preferred_element_type=jnp.float32)
        act = jax.nn.silu(pre).astype(jnp.bfloat16)
        back = contract_cols(upper, weight_out)
        pre_grad = (back * silu_slope(pre)).astype(jnp.bfloat16)
        passed = (upper.astype(jnp.float32) + contract_cols(pre_grad, weight_in)).astype(
            jnp.bfloat16
        )
        total_in, total_out = lax.cond(
            active, accumulate, keep_totals, ((total_in, total_out), inputs, pre_grad, act, upper)
        )
        incoming = passed_along(passed, "section", -1)
        return (incoming, total_in, total_out)

    start = (
        jnp.zeros((tokens, width), jnp.bfloat16),
        jnp.zeros((width, order), jnp.float32),
        jnp.zeros((order, width), jnp.float32),
    )
    final = lax.fori_loop(0, section_count + micro - 1, tick, start)
    part_in = final[1].astype(jnp.bfloat16).reshape(row_blocks, order, order)
    part_out = final[2].astype(jnp.bfloat16).reshape(order, row_blocks, order).transpose(1, 0, 2)
    all_blocks = jnp.concatenate([part_in, part_out], axis=0)
    lists = owned_blocks[0]
    slot_index = jnp.arange(slots, dtype=jnp.int32)
    live = slot_index[None, :] < owned_count[0][:, None]
    my_index = lax.axis_index("dp")
    my_live = lax.dynamic_index_in_dim(live, my_index, 0, keepdims=False)
    my_lists = lax.dynamic_index_in_dim(lists, my_index, 0, keepdims=False)
    outgoing = jnp.take(all_blocks, lists.reshape(-1), axis=0).reshape(owners, slots, order, order)
    outgoing = jnp.where(live[:, :, None, None], outgoing, jnp.zeros_like(outgoing))
    arrived = lax.all_to_all(outgoing, "dp", split_axis=0, concat_axis=0, tiled=True)
    grad_low = (jnp.sum(arrived.astype(jnp.float32), axis=0) / owners).astype(jnp.bfloat16)
    grad_low = lax.optimization_barrier(grad_low)
    grad = grad_low.astype(jnp.float32)
    first = jnp.einsum(
        "kij,kjl->kil", left_root[0, 0], grad_low, preferred_element_type=jnp.float32
    )
    right = right_root[0, 0].astype(jnp.float32)
    precond = jnp.einsum("kij,kjl->kil", first, right, precision=lax.Precision.HIGHEST)
    grad_sq = jnp.sum(grad * grad, axis=(1, 2))
    pre_sq = jnp.sum(precond * precond, axis=(1, 2))
    direction = precond * (jnp.sqrt(grad_sq) * lax.rsqrt(pre_sq + 1e-06))[:, None, None]
    moved = MOMENTUM_DECAY * momentum[0, 0] + direction
    new_mom = jnp.where(my_live[:, None, None], moved, momentum[0, 0])
    search = new_mom.astype(jnp.bfloat16)
    keep_count = row_blocks // lax.axis_size("dp")
    home_offsets = jnp.arange(keep_count, dtype=jnp.int32)
    device_ids = jnp.arange(owners, dtype=jnp.int32)[:, None] * keep_count + home_offsets[None, :]
    dest_ids = jnp.concatenate([device_ids, row_blocks + device_ids], axis=1)
    selector = (dest_ids[:, :, None] == my_lists[None, None, :]) & my_live[None, None, :]
    selector = selector.astype(jnp.bfloat16).reshape(owners * 2 * keep_count, slots)
    packed = jnp.dot(
        selector, search.reshape(slots, order * order), preferred_element_type=jnp.float32
    )
    packed = packed.astype(jnp.bfloat16).reshape(owners, 2 * keep_count, order, order)
    received = lax.all_to_all(packed, "dp", split_axis=0, concat_axis=0, tiled=True)
    placed = jnp.sum(received.astype(jnp.float32), axis=0).astype(jnp.bfloat16)
    search_in = placed[:keep_count].reshape(keep_count * order, order)[None]
    search_out = placed[keep_count:].transpose(1, 0, 2).reshape(order, keep_count * order)[None]
    return (new_mom[None, None], search_in, search_out)


def solution(mesh):
    placed = (
        P("section", None, "dp", None),
        P(None, "dp", None),
        P("section", None, None),
        P("section", None, None),
        P("section", "dp", None, None, None),
        P("section", "dp", None, None, None),
        P("section", "dp", None, None, None),
        P("section", None, None),
        P("section", None),
    )
    return jax.shard_map(
        on_device,
        mesh=mesh,
        in_specs=placed,
        out_specs=(
            P("section", "dp", None, None, None),
            P("section", "dp", None),
            P("section", None, "dp"),
        ),
        check_vma=False,
    )
```

profile of v0, /device:TPU:1, one launch (start us, length us, event | category | flops | bytes accessed | tf_op | source)
XLA Modules:
  0.0 440.5 jit_solution(706161644965138421)
XLA Ops:
  2.1 1.5 broadcast_in_dim.56
  3.6 1.5 broadcast_in_dim.57
  6.0 302.7 %while.19 = (s32[]{:T(128)}, bf16[64,4096]{1,0:T(8,128)(2,1)}, f32[4096,128]{1,0:T(8,128)}, f32[128,4096]{1,0:T(8,128)}, pred[]{:T(512)}, /*index=5*/s32[]{:T(12...) while((s32[]{:T(128)}, bf16[64,4096]{1,0:T(8,128)(2,1)}, ...), condition=%wide.region_3.4_spmd, body=%wide.region_0.3_spmd.sunk | while | flops 337756160 | bytes 40518040 | solution.py:81
  10.4 1.3 collective-permute-start
  11.7 9.9 %collective-permute-done = bf16[64,4096]{1,0:T(8,128)(2,1)} collective-permute-done((bf16[64,4096]{1,0:T(8,128)(2,1)}, bf16[64,4096]{1,0:T(8,128)(2,1)}, u32[]{:S(2)}, u32[]{:S(2)}) %collective-permute-start) | collective-permute-done | bytes 524320 | tf_op jit(solution)/shard_map/while/body/eval_jaxpr/ppermute | solution.py:12
  24.8 1.3 fusion.45
  26.0 1.3 collective-permute-start
  27.4 17.6 %collective-permute-done = bf16[64,4096]{1,0:T(8,128)(2,1)} collective-permute-done((bf16[64,4096]{1,0:T(8,128)(2,1)}, bf16[64,4096]{1,0:T(8,128)(2,1)}, u32[]{:S(2)}, u32[]{:S(2)}) %collective-permute-start) | collective-permute-done | bytes 524320 | tf_op jit(solution)/shard_map/while/body/eval_jaxpr/ppermute | solution.py:12
  49.3 1.3 collective-permute-start
  50.6 13.3 %collective-permute-done = bf16[64,4096]{1,0:T(8,128)(2,1)} collective-permute-done((bf16[64,4096]{1,0:T(8,128)(2,1)}, bf16[64,4096]{1,0:T(8,128)(2,1)}, u32[]{:S(2)}, u32[]{:S(2)}) %collective-permute-start) | collective-permute-done | bytes 524320 | tf_op jit(solution)/shard_map/while/body/eval_jaxpr/ppermute | solution.py:12
  67.1 1.3 fusion.45
  69.7 13.7 %collective-permute-done = bf16[64,4096]{1,0:T(8,128)(2,1)} collective-permute-done((bf16[64,4096]{1,0:T(8,128)(2,1)}, bf16[64,4096]{1,0:T(8,128)(2,1)}, u32[]{:S(2)}, u32[]{:S(2)}) %collective-permute-start) | collective-permute-done | bytes 524320 | tf_op jit(solution)/shard_map/while/body/eval_jaxpr/ppermute | solution.py:12
  89.0 11.4 %collective-permute-done = bf16[64,4096]{1,0:T(8,128)(2,1)} collective-permute-done((bf16[64,4096]{1,0:T(8,128)(2,1)}, bf16[64,4096]{1,0:T(8,128)(2,1)}, u32[]{:S(2)}, u32[]{:S(2)}) %collective-permute-start) | collective-permute-done | bytes 524320 | tf_op jit(solution)/shard_map/while/body/eval_jaxpr/ppermute | solution.py:12
  106.1 10.5 %collective-permute-done = bf16[64,4096]{1,0:T(8,128)(2,1)} collective-permute-done((bf16[64,4096]{1,0:T(8,128)(2,1)}, bf16[64,4096]{1,0:T(8,128)(2,1)}, u32[]{:S(2)}, u32[]{:S(2)}) %collective-permute-start) | collective-permute-done | bytes 524320 | tf_op jit(solution)/shard_map/while/body/eval_jaxpr/ppermute | solution.py:12
  119.8 1.3 fusion.45
  122.4 9.3 %collective-permute-done = bf16[64,4096]{1,0:T(8,128)(2,1)} collective-permute-done((bf16[64,4096]{1,0:T(8,128)(2,1)}, bf16[64,4096]{1,0:T(8,128)(2,1)}, u32[]{:S(2)}, u32[]{:S(2)}) %collective-permute-start) | collective-permute-done | bytes 524320 | tf_op jit(solution)/shard_map/while/body/eval_jaxpr/ppermute | solution.py:12
  134.7 1.3 fusion.45
  137.3 9.6 %collective-permute-done = bf16[64,4096]{1,0:T(8,128)(2,1)} collective-permute-done((bf16[64,4096]{1,0:T(8,128)(2,1)}, bf16[64,4096]{1,0:T(8,128)(2,1)}, u32[]{:S(2)}, u32[]{:S(2)}) %collective-permute-start) | collective-permute-done | bytes 524320 | tf_op jit(solution)/shard_map/while/body/eval_jaxpr/ppermute | solution.py:12
  152.6 9.8 %collective-permute-done = bf16[64,4096]{1,0:T(8,128)(2,1)} collective-permute-done((bf16[64,4096]{1,0:T(8,128)(2,1)}, bf16[64,4096]{1,0:T(8,128)(2,1)}, u32[]{:S(2)}, u32[]{:S(2)}) %collective-permute-start) | collective-permute-done | bytes 524320 | tf_op jit(solution)/shard_map/while/body/eval_jaxpr/ppermute | solution.py:12
  165.6 1.3 fusion.45
  168.2 10.1 %collective-permute-done = bf16[64,4096]{1,0:T(8,128)(2,1)} collective-permute-done((bf16[64,4096]{1,0:T(8,128)(2,1)}, bf16[64,4096]{1,0:T(8,128)(2,1)}, u32[]{:S(2)}, u32[]{:S(2)}) %collective-permute-start) | collective-permute-done | bytes 524320 | tf_op jit(solution)/shard_map/while/body/eval_jaxpr/ppermute | solution.py:12
  181.4 1.3 fusion.45
  184.0 10.1 %collective-permute-done = bf16[64,4096]{1,0:T(8,128)(2,1)} collective-permute-done((bf16[64,4096]{1,0:T(8,128)(2,1)}, bf16[64,4096]{1,0:T(8,128)(2,1)}, u32[]{:S(2)}, u32[]{:S(2)}) %collective-permute-start) | collective-permute-done | bytes 524320 | tf_op jit(solution)/shard_map/while/body/eval_jaxpr/ppermute | solution.py:12
  197.3 1.3 fusion.45
  199.9 10.1 %collective-permute-done = bf16[64,4096]{1,0:T(8,128)(2,1)} collective-permute-done((bf16[64,4096]{1,0:T(8,128)(2,1)}, bf16[64,4096]{1,0:T(8,128)(2,1)}, u32[]{:S(2)}, u32[]{:S(2)}) %collective-permute-start) | collective-permute-done | bytes 524320 | tf_op jit(solution)/shard_map/while/body/eval_jaxpr/ppermute | solution.py:12
  213.1 1.3 fusion.45
  215.7 11.4 %collective-permute-done = bf16[64,4096]{1,0:T(8,128)(2,1)} collective-permute-done((bf16[64,4096]{1,0:T(8,128)(2,1)}, bf16[64,4096]{1,0:T(8,128)(2,1)}, u32[]{:S(2)}, u32[]{:S(2)}) %collective-permute-start) | collective-permute-done | bytes 524320 | tf_op jit(solution)/shard_map/while/body/eval_jaxpr/ppermute | solution.py:12
  230.2 1.3 fusion.45
  232.8 12.8 %collective-permute-done = bf16[64,4096]{1,0:T(8,128)(2,1)} collective-permute-done((bf16[64,4096]{1,0:T(8,128)(2,1)}, bf16[64,4096]{1,0:T(8,128)(2,1)}, u32[]{:S(2)}, u32[]{:S(2)}) %collective-permute-start) | collective-permute-done | bytes 524320 | tf_op jit(solution)/shard_map/while/body/eval_jaxpr/ppermute | solution.py:12
  251.3 14.2 %collective-permute-done = bf16[64,4096]{1,0:T(8,128)(2,1)} collective-permute-done((bf16[64,4096]{1,0:T(8,128)(2,1)}, bf16[64,4096]{1,0:T(8,128)(2,1)}, u32[]{:S(2)}, u32[]{:S(2)}) %collective-permute-start) | collective-permute-done | bytes 524320 | tf_op jit(solution)/shard_map/while/body/eval_jaxpr/ppermute | solution.py:12
  268.6 1.3 fusion.45
  271.2 5.6 %conditional.2 = ((f32[4096,128]{1,0:T(8,128)}, f32[128,4096]{1,0:T(8,128)})) conditional(s32[]{:T(128)} %convert_element_type.97, (f32[4096,128]{1,0:T(8,128)}, f32[128,4096]{1,0:T(8,128)}) %tuple.54, (bf16[64,4096]{1,0:T(8,128)(2,1)S(1)}, bf16[64,128]{1,0:T(8,128)(2,1)S(1)}, f32[4096,128]{1,0:T(8,128)}, bf16[64,128]{1,0:T(8,128)(2,1)S(1)}, ...), branch_computations={%region_1.1_spmd, %region_2.2_spmd} | conditional | flops 135266304 | bytes 26247248 | solution.py:70
  271.2 3.5 convolution_add_fusion
  275.4 1.3 copy-done.3
  276.8 9.7 %collective-permute-done = bf16[64,4096]{1,0:T(8,128)(2,1)} collective-permute-done((bf16[64,4096]{1,0:T(8,128)(2,1)}, bf16[64,4096]{1,0:T(8,128)(2,1)}, u32[]{:S(2)}, u32[]{:S(2)}) %collective-permute-start) | collective-permute-done | bytes 524320 | tf_op jit(solution)/shard_map/while/body/eval_jaxpr/ppermute | solution.py:12
  292.2 5.6 %conditional.2 = ((f32[4096,128]{1,0:T(8,128)}, f32[128,4096]{1,0:T(8,128)})) conditional(s32[]{:T(128)} %convert_element_type.97, (f32[4096,128]{1,0:T(8,128)}, f32[128,4096]{1,0:T(8,128)}) %tuple.54, (bf16[64,4096]{1,0:T(8,128)(2,1)S(1)}, bf16[64,128]{1,0:T(8,128)(2,1)S(1)}, f32[4096,128]{1,0:T(8,128)}, bf16[64,128]{1,0:T(8,128)(2,1)S(1)}, ...), branch_computations={%region_1.1_spmd, %region_2.2_spmd} | conditional | flops 135266304 | bytes 26247248 | solution.py:70
  292.2 3.5 convolution_add_fusion
  296.4 1.3 copy-done.3
  297.8 11.0 %collective-permute-done = bf16[64,4096]{1,0:T(8,128)(2,1)} collective-permute-done((bf16[64,4096]{1,0:T(8,128)(2,1)}, bf16[64,4096]{1,0:T(8,128)(2,1)}, u32[]{:S(2)}, u32[]{:S(2)}) %collective-permute-start) | collective-permute-done | bytes 524320 | tf_op jit(solution)/shard_map/while/body/eval_jaxpr/ppermute | solution.py:12
  308.7 2.0 copy.23
  310.7 1.3 copy.24
  312.9 1.4 pad_maximum_fusion
  314.3 3.1 gather_fusion
  317.3 3.9 select_select_fusion
  321.2 25.2 %all-to-all-start = ((bf16[32,4,128,128]{3,2,1,0:T(8,128)(2,1)}), bf16[32,4,128,128]{3,2,1,0:T(8,128)(2,1)}, u32[]{:S(2)}, u32[]{:S(2)}) async-start(bf16[32,4,128,128]{3,2,1,0:T(8,128)(2,1)} %select_select_fusion), calls=%async_computation | async-start | bytes 8388608 | tf_op jit(solution)/shard_map/all_to_all | solution.py:93
  346.9 51.7 %all-to-all-done = bf16[32,4,128,128]{3,2,1,0:T(8,128)(2,1)} async-done(((bf16[32,4,128,128]{3,2,1,0:T(8,128)(2,1)}), bf16[32,4,128,128]{3,2,1,0:T(8,128)(2,1)}, u32[]{:S(2)}, u32[]{:S(2)}) %all-to-all-start) | async-done | bytes 4194336 | tf_op jit(solution)/shard_map/all_to_all | solution.py:93
  398.6 3.0 convert_reduce_fusion
  404.5 35.1 %all_to_all.10 = bf16[32,2,128,128]{3,2,1,0:T(8,128)(2,1)S(1)} all-to-all(bf16[32,2,128,128]{3,2,1,0:T(8,128)(2,1)S(1)} %bitcast.81), channel_id=1, replica_groups=mesh['section'=16,'dp'=32] {'dp'}, dimensions={0} | all-to-all | bytes 4194304 | tf_op jit(solution)/shard_map/all_to_all | solution.py:118
  (188 shorter events, 88.3 us)
Async XLA Ops:
  0.6 401.3 %copy-start = (bf16[1,1,4,128,128]{4,3,2,1,0:T(8,128)(2,1)S(1)}, bf16[1,1,4,128,128]{4,3,2,1,0:T(8,128)(2,1)}, u32[]{:S(2)}) copy-start(bf16[1,1,4,128,128]{4,3,2,1,0:T(8,128)(2,1)} %param.18) | copy-start | bytes 393220
  2.1 3.9 copy-start.1
  2.1 3.9 copy-start.5
  6.0 1.5 copy-start.6
  10.4 11.2 %collective-permute-start = (bf16[64,4096]{1,0:T(8,128)(2,1)}, bf16[64,4096]{1,0:T(8,128)(2,1)}, u32[]{:S(2)}, u32[]{:S(2)}) collective-permute-start(bf16[64,4096]{1,0:T(8,128)(2,1)} %fusion.45), channel_id=1, source_target_pairs={{32,0},{64,32},{96,64},{128,96},{160,128},{192,160},{224,192},{256... | collective-permute-start | bytes 1572872 | tf_op jit(solution)/shard_map/while/body/eval_jaxpr/ppermute | solution.py:12
  21.6 1.5 copy-start.6
  26.0 18.9 %collective-permute-start = (bf16[64,4096]{1,0:T(8,128)(2,1)}, bf16[64,4096]{1,0:T(8,128)(2,1)}, u32[]{:S(2)}, u32[]{:S(2)}) collective-permute-start(bf16[64,4096]{1,0:T(8,128)(2,1)} %fusion.45), channel_id=1, source_target_pairs={{32,0},{64,32},{96,64},{128,96},{160,128},{192,160},{224,192},{256... | collective-permute-start | bytes 1572872 | tf_op jit(solution)/shard_map/while/body/eval_jaxpr/ppermute | solution.py:12
  44.9 1.5 copy-start.6
  49.3 14.6 %collective-permute-start = (bf16[64,4096]{1,0:T(8,128)(2,1)}, bf16[64,4096]{1,0:T(8,128)(2,1)}, u32[]{:S(2)}, u32[]{:S(2)}) collective-permute-start(bf16[64,4096]{1,0:T(8,128)(2,1)} %fusion.45), channel_id=1, source_target_pairs={{32,0},{64,32},{96,64},{128,96},{160,128},{192,160},{224,192},{256... | collective-permute-start | bytes 1572872 | tf_op jit(solution)/shard_map/while/body/eval_jaxpr/ppermute | solution.py:12
  63.9 1.5 copy-start.6
  68.3 15.0 %collective-permute-start = (bf16[64,4096]{1,0:T(8,128)(2,1)}, bf16[64,4096]{1,0:T(8,128)(2,1)}, u32[]{:S(2)}, u32[]{:S(2)}) collective-permute-start(bf16[64,4096]{1,0:T(8,128)(2,1)} %fusion.45), channel_id=1, source_target_pairs={{32,0},{64,32},{96,64},{128,96},{160,128},{192,160},{224,192},{256... | collective-permute-start | bytes 1572872 | tf_op jit(solution)/shard_map/while/body/eval_jaxpr/ppermute | solution.py:12
  83.3 1.5 copy-start.6
  87.7 12.7 %collective-permute-start = (bf16[64,4096]{1,0:T(8,128)(2,1)}, bf16[64,4096]{1,0:T(8,128)(2,1)}, u32[]{:S(2)}, u32[]{:S(2)}) collective-permute-start(bf16[64,4096]{1,0:T(8,128)(2,1)} %fusion.45), channel_id=1, source_target_pairs={{32,0},{64,32},{96,64},{128,96},{160,128},{192,160},{224,192},{256... | collective-permute-start | bytes 1572872 | tf_op jit(solution)/shard_map/while/body/eval_jaxpr/ppermute | solution.py:12
  100.4 1.5 copy-start.6
  104.8 11.9 %collective-permute-start = (bf16[64,4096]{1,0:T(8,128)(2,1)}, bf16[64,4096]{1,0:T(8,128)(2,1)}, u32[]{:S(2)}, u32[]{:S(2)}) collective-permute-start(bf16[64,4096]{1,0:T(8,128)(2,1)} %fusion.45), channel_id=1, source_target_pairs={{32,0},{64,32},{96,64},{128,96},{160,128},{192,160},{224,192},{256... | collective-permute-start | bytes 1572872 | tf_op jit(solution)/shard_map/while/body/eval_jaxpr/ppermute | solution.py:12
  116.7 1.5 copy-start.6
  121.1 10.6 %collective-permute-start = (bf16[64,4096]{1,0:T(8,128)(2,1)}, bf16[64,4096]{1,0:T(8,128)(2,1)}, u32[]{:S(2)}, u32[]{:S(2)}) collective-permute-start(bf16[64,4096]{1,0:T(8,128)(2,1)} %fusion.45), channel_id=1, source_target_pairs={{32,0},{64,32},{96,64},{128,96},{160,128},{192,160},{224,192},{256... | collective-permute-start | bytes 1572872 | tf_op jit(solution)/shard_map/while/body/eval_jaxpr/ppermute | solution.py:12
  131.6 1.5 copy-start.6
  136.0 10.9 %collective-permute-start = (bf16[64,4096]{1,0:T(8,128)(2,1)}, bf16[64,4096]{1,0:T(8,128)(2,1)}, u32[]{:S(2)}, u32[]{:S(2)}) collective-permute-start(bf16[64,4096]{1,0:T(8,128)(2,1)} %fusion.45), channel_id=1, source_target_pairs={{32,0},{64,32},{96,64},{128,96},{160,128},{192,160},{224,192},{256... | collective-permute-start | bytes 1572872 | tf_op jit(solution)/shard_map/while/body/eval_jaxpr/ppermute | solution.py:12
  146.9 1.5 copy-start.6
  151.3 11.2 %collective-permute-start = (bf16[64,4096]{1,0:T(8,128)(2,1)}, bf16[64,4096]{1,0:T(8,128)(2,1)}, u32[]{:S(2)}, u32[]{:S(2)}) collective-permute-start(bf16[64,4096]{1,0:T(8,128)(2,1)} %fusion.45), channel_id=1, source_target_pairs={{32,0},{64,32},{96,64},{128,96},{160,128},{192,160},{224,192},{256... | collective-permute-start | bytes 1572872 | tf_op jit(solution)/shard_map/while/body/eval_jaxpr/ppermute | solution.py:12
  162.5 1.5 copy-start.6
  166.9 11.4 %collective-permute-start = (bf16[64,4096]{1,0:T(8,128)(2,1)}, bf16[64,4096]{1,0:T(8,128)(2,1)}, u32[]{:S(2)}, u32[]{:S(2)}) collective-permute-start(bf16[64,4096]{1,0:T(8,128)(2,1)} %fusion.45), channel_id=1, source_target_pairs={{32,0},{64,32},{96,64},{128,96},{160,128},{192,160},{224,192},{256... | collective-permute-start | bytes 1572872 | tf_op jit(solution)/shard_map/while/body/eval_jaxpr/ppermute | solution.py:12
  178.3 1.5 copy-start.6
  182.7 11.4 %collective-permute-start = (bf16[64,4096]{1,0:T(8,128)(2,1)}, bf16[64,4096]{1,0:T(8,128)(2,1)}, u32[]{:S(2)}, u32[]{:S(2)}) collective-permute-start(bf16[64,4096]{1,0:T(8,128)(2,1)} %fusion.45), channel_id=1, source_target_pairs={{32,0},{64,32},{96,64},{128,96},{160,128},{192,160},{224,192},{256... | collective-permute-start | bytes 1572872 | tf_op jit(solution)/shard_map/while/body/eval_jaxpr/ppermute | solution.py:12
  194.1 1.5 copy-start.6
  198.5 11.4 %collective-permute-start = (bf16[64,4096]{1,0:T(8,128)(2,1)}, bf16[64,4096]{1,0:T(8,128)(2,1)}, u32[]{:S(2)}, u32[]{:S(2)}) collective-permute-start(bf16[64,4096]{1,0:T(8,128)(2,1)} %fusion.45), channel_id=1, source_target_pairs={{32,0},{64,32},{96,64},{128,96},{160,128},{192,160},{224,192},{256... | collective-permute-start | bytes 1572872 | tf_op jit(solution)/shard_map/while/body/eval_jaxpr/ppermute | solution.py:12
  210.0 1.5 copy-start.6
  214.4 12.7 %collective-permute-start = (bf16[64,4096]{1,0:T(8,128)(2,1)}, bf16[64,4096]{1,0:T(8,128)(2,1)}, u32[]{:S(2)}, u32[]{:S(2)}) collective-permute-start(bf16[64,4096]{1,0:T(8,128)(2,1)} %fusion.45), channel_id=1, source_target_pairs={{32,0},{64,32},{96,64},{128,96},{160,128},{192,160},{224,192},{256... | collective-permute-start | bytes 1572872 | tf_op jit(solution)/shard_map/while/body/eval_jaxpr/ppermute | solution.py:12
  227.1 1.5 copy-start.6
  231.5 14.1 %collective-permute-start = (bf16[64,4096]{1,0:T(8,128)(2,1)}, bf16[64,4096]{1,0:T(8,128)(2,1)}, u32[]{:S(2)}, u32[]{:S(2)}) collective-permute-start(bf16[64,4096]{1,0:T(8,128)(2,1)} %fusion.45), channel_id=1, source_target_pairs={{32,0},{64,32},{96,64},{128,96},{160,128},{192,160},{224,192},{256... | collective-permute-start | bytes 1572872 | tf_op jit(solution)/shard_map/while/body/eval_jaxpr/ppermute | solution.py:12
  245.6 1.5 copy-start.6
  250.0 15.5 %collective-permute-start = (bf16[64,4096]{1,0:T(8,128)(2,1)}, bf16[64,4096]{1,0:T(8,128)(2,1)}, u32[]{:S(2)}, u32[]{:S(2)}) collective-permute-start(bf16[64,4096]{1,0:T(8,128)(2,1)} %fusion.45), channel_id=1, source_target_pairs={{32,0},{64,32},{96,64},{128,96},{160,128},{192,160},{224,192},{256... | collective-permute-start | bytes 1572872 | tf_op jit(solution)/shard_map/while/body/eval_jaxpr/ppermute | solution.py:12
  265.5 1.5 copy-start.6
  269.9 16.6 %collective-permute-start = (bf16[64,4096]{1,0:T(8,128)(2,1)}, bf16[64,4096]{1,0:T(8,128)(2,1)}, u32[]{:S(2)}, u32[]{:S(2)}) collective-permute-start(bf16[64,4096]{1,0:T(8,128)(2,1)} %fusion.45), channel_id=1, source_target_pairs={{32,0},{64,32},{96,64},{128,96},{160,128},{192,160},{224,192},{256... | collective-permute-start | bytes 1572872 | tf_op jit(solution)/shard_map/while/body/eval_jaxpr/ppermute | solution.py:12
  271.2 3.5 copy-start.2
  275.4 1.3 copy-start.3
  286.5 1.5 copy-start.6
  290.9 17.8 %collective-permute-start = (bf16[64,4096]{1,0:T(8,128)(2,1)}, bf16[64,4096]{1,0:T(8,128)(2,1)}, u32[]{:S(2)}, u32[]{:S(2)}) collective-permute-start(bf16[64,4096]{1,0:T(8,128)(2,1)} %fusion.45), channel_id=1, source_target_pairs={{32,0},{64,32},{96,64},{128,96},{160,128},{192,160},{224,192},{256... | collective-permute-start | bytes 1572872 | tf_op jit(solution)/shard_map/while/body/eval_jaxpr/ppermute | solution.py:12
  292.2 3.5 copy-start.2
  296.4 1.3 copy-start.3
  308.7 3.3 copy-start.4
  312.0 0.7 copy-start.10
  321.2 25.2 %copy-start.9 = (s32[1,32,4]{1,2,0:T(4,128)S(1)}, s32[1,32,4]{1,2,0:T(4,128)}, u32[]{:S(2)}) copy-start(s32[1,32,4]{1,2,0:T(4,128)} %param.20) | copy-start | bytes 1540
  321.2 77.4 %all-to-all-start = ((bf16[32,4,128,128]{3,2,1,0:T(8,128)(2,1)}), bf16[32,4,128,128]{3,2,1,0:T(8,128)(2,1)}, u32[]{:S(2)}, u32[]{:S(2)}) async-start(bf16[32,4,128,128]{3,2,1,0:T(8,128)(2,1)} %select_select_fusion), calls=%async_computation | async-start | bytes 8388608 | tf_op jit(solution)/shard_map/all_to_all | solution.py:93
  346.8 54.9 %copy-start.8 = (bf16[1,1,4,128,128]{4,3,2,1,0:T(8,128)(2,1)S(1)}, bf16[1,1,4,128,128]{4,3,2,1,0:T(8,128)(2,1)}, u32[]{:S(2)}) copy-start(bf16[1,1,4,128,128]{4,3,2,1,0:T(8,128)(2,1)} %param.17) | copy-start | bytes 393220
  346.9 55.5 %copy-start.7 = (f32[1,1,4,128,128]{4,3,2,1,0:T(8,128)S(1)}, f32[1,1,4,128,128]{4,3,2,1,0:T(8,128)}, u32[]{:S(2)}) copy-start(f32[1,1,4,128,128]{4,3,2,1,0:T(8,128)} %param.19) | copy-start | bytes 786436
where the time goes:
time: 446 us; the launch traced here: 441 us
  waiting for transfers between devices  246 us (55%)
  starting transfers between devices  46.9 us (11%)
  matrix products  45.2 us (10%)
  local copies, waits for them, and re-layouts  35.8 us (8%)
  blocking collectives  35.1 us (8%)
  other arithmetic  29.3 us (7%)
    ppermute x17, waiting for transfers between devices, passed_along(): lax.ppermute(value, axis, [(source, source + steps) for source in range(i...  194 us
    all_to_all x1, waiting for transfers between devices, on_device(): lax.all_to_all(outgoing, 'dp', split_axis=0, concat_axis=0, tiled=True)  51.7 us
    all_to_all x1, blocking collectives, on_device(): lax.all_to_all(packed, 'dp', split_axis=0, concat_axis=0, tiled=True)  35.1 us
    dot_general x34, matrix products, contract_cols(): lax.dot_general(left_side, right_side, (((1,), (1,)), ((), ())), preferre...  29.9 us
    all_to_all x1, starting transfers between devices, on_device(): lax.all_to_all(outgoing, 'dp', split_axis=0, concat_axis=0, tiled=True)  25.2 us
    ppermute x17, starting transfers between devices, passed_along(): lax.ppermute(value, axis, [(source, source + steps) for source in range(i...  21.8 us
    squeeze x17, local copies, waits for them, and re-layouts, tick(): inputs = lax.dynamic_index_in_dim(inputs_all, chosen, 0, keepdims=False)  19.8 us
    select_n x17, other arithmetic, tick(): upper = jnp.where(section_index == section_count - 1, given, incoming)  18.8 us
  transfers between devices with their start and end apart: 18, of which 18 were waited for; matrix products, arithmetic and copies ran while one was open for 2% of the time, Pallas kernels for 0%

commit v1 on v0

v1 whole, which is shorter than its diff:
```python
import functools

import jax
import jax.numpy as jnp
from jax import lax
from jax.experimental import pallas as pl
from jax.experimental.pallas import tpu as pltpu
from jax.sharding import PartitionSpec as P

MOMENTUM_DECAY = 0.9
MESH = pl.DeviceIdType.MESH
BF16 = jnp.bfloat16
F32 = jnp.float32
COPIES = 160


def dot_nn(a, b):
    return lax.dot_general(a, b, (((1,), (0,)), ((), ())), preferred_element_type=F32)


def dot_nt(a, b):
    return lax.dot_general(a, b, (((1,), (1,)), ((), ())), preferred_element_type=F32)


def silu_slope(values):
    sigma = jax.nn.sigmoid(values)
    return sigma * (1.0 + values * (1.0 - sigma))


def kernel(
    sections,
    x_ref, gl_ref, win_ref, wout_ref, left_ref, right_ref, mom_ref, lists, count,
    newmom_ref, search_in_ref, search_out_ref,
    wz, pg, slope, acc, act_t,
    m_p, m_rc, m_q, m_ra, m_t, m_rb, m_o,
    c_p, c_rc, c_q, c_ra, c_t, c_rb, c_o,
    i_p, i_rc, i_q, i_ra, i_t, i_rb,
    o_p, o_rc, o_q, o_ra, o_t, o_rb,
    r_x, r_pk, r_rk, r_sum, r_rc, r_home,
    d_x, d_pk, d_rk,
    send, recv, z_send, z_recv, p_send, p_recv,
):
    s = lax.axis_index("section")
    dp = lax.axis_index("dp")
    c = lax.rem(dp, 2)
    y = lax.rem(dp // 2, 4)
    x = dp // 8
    last = sections - 1
    first_of = (x, y)
    second_of = (y, x)
    wide = s <= last - 9
    ids = {}

    def sid(key):
        return ids.setdefault(key, len(ids))

    def device(h, a, b):
        return (a * 4 + b) * 2 + c if h == 0 else (b * 4 + a) * 2 + c

    def remote(key, source, target, peer):
        number = sid(key)
        return pltpu.make_async_remote_copy(
            src_ref=source, dst_ref=target, send_sem=send.at[number], recv_sem=recv.at[number],
            device_id={"dp": peer}, device_id_type=MESH,
        )

    sibling = dp + 1 - 2 * c

    def peer_first(h, i):
        a = lax.rem(first_of[h] + i, 4)
        return a, device(h, a, second_of[h])

    def peer_second(h, i):
        b = lax.rem(second_of[h] + i, 4)
        return b, device(h, first_of[h], b)

    def go(copies):
        for copy in copies:
            copy.start()

    def land(copies):
        for copy in copies:
            copy.wait_recv()

    def sent(copies):
        for copy in copies:
            copy.wait_send()

    barrier = pltpu.get_barrier_semaphore()
    greeted = [sibling]
    for h in range(2):
        for i in range(1, 4):
            greeted.append(peer_first(h, i)[1])
    for peer in greeted:
        pl.semaphore_signal(barrier, inc=1, device_id={"dp": peer}, device_id_type=MESH)
    below = lax.rem(s + last, sections)
    above = lax.rem(s + 1, sections)
    for peer in (below, above):
        pl.semaphore_signal(barrier, inc=1, device_id={"section": peer}, device_id_type=MESH)
    pl.semaphore_wait(barrier, 9)

    def slice_copy(index):
        return pltpu.make_async_remote_copy(
            src_ref=wz.at[index], dst_ref=wz.at[index],
            send_sem=z_send.at[index], recv_sem=z_recv.at[index],
            device_id={"section": below}, device_id_type=MESH,
        )

    def pass_copy(index):
        return pltpu.make_async_remote_copy(
            src_ref=pg.at[index], dst_ref=pg.at[index],
            send_sem=p_send.at[index], recv_sem=p_recv.at[index],
            device_id={"section": below}, device_id_type=MESH,
        )

    my_columns = pl.ds(pl.multiple_of(dp * 128, 128), 128)
    wz[s] = win_ref[my_columns, :]

    @pl.when(s > 0)
    def _():
        slice_copy(s).start()

    for h in range(2):
        for k in range(4):
            rows = pl.ds(h * 64, 64)
            at = first_of[h] * 4 + k
            r_x[h, at, 0] = left_ref[k, rows]
            r_x[h, at, 1] = right_ref[k, rows]
            r_x[h, at, 2] = mom_ref[k, rows].astype(BF16)

    def roots_first():
        copies = []
        for h in range(2):
            mine = r_x.at[h, pl.ds(first_of[h] * 4, 4)]
            for i in range(1, 4):
                copies.append(remote(("ra", h, i), mine, mine, peer_first(h, i)[1]))
        return copies

    def roots_second():
        copies = []
        for h in range(2):
            for i in range(1, 4):
                b, peer = peer_second(h, i)
                copies.append(remote(("rb", h, i), r_pk.at[h, b], r_rk.at[h, i - 1], peer))
        return copies

    def roots_pair():
        return [remote(("rc",), r_sum.at[:, 1 - c], r_rc, sibling)]

    def roots_pack():
        land(roots_first())
        for h in range(2):
            def target(t, carry):
                b, core, kind = t // 4, lax.rem(t // 2, 2), lax.rem(t, 2)
                if h == 0:
                    place = (first_of[h] * 4 + b) * 2 + core
                else:
                    place = (b * 4 + first_of[h]) * 2 + core
                block = kind * 32 + place
                index = jnp.int32(0)
                found = jnp.int32(0)
                for a in range(4):
                    owner = device(h, a, second_of[h])
                    held = count[owner]
                    for k in range(4):
                        hit = (lists[owner * 4 + k] == block) & (held > k)
                        index = index + jnp.where(hit, a * 4 + k, 0)
                        found = found + jnp.where(hit, 1, 0)
                value = r_x[h, index]
                r_pk[h, b, core, kind] = jnp.where(found > 0, value, jnp.zeros_like(value))
                return carry
            lax.fori_loop(0, 16, target, 0)
        go(roots_second())

    pl.when(s <= 7)(lambda: go(roots_first()))

    pre = dot_nn(x_ref[...], win_ref[...])
    slope[...] = silu_slope(pre)
    act = jax.nn.silu(pre)
    act_t[...] = act.T.astype(BF16)
    acc[...] = dot_nt(gl_ref[...], wout_ref[...])

    @pl.when(s == last)
    def _():
        pg[s] = (acc[...] * slope[...]).astype(BF16)
        pass_copy(s).start()

    m_p[...] = jnp.zeros_like(m_p)
    c_p[...] = jnp.zeros_like(c_p)

    def relay(k, carry):
        index = s + 1 + k
        copy = slice_copy(index)
        copy.wait_recv()
        pl.when(s > 0)(lambda: copy.start())
        product = dot_nn(wout_ref[:, my_columns], wz[index])
        m_p[k] = product.T.astype(BF16).reshape(4, 2, 16, 128)
        return carry

    lax.fori_loop(0, last - s, relay, 0)

    class Sum:
        def __init__(self, name, p, rc, q, ra, t, rb, o):
            self.name, self.p, self.rc, self.q, self.ra = name, p, rc, q, ra
            self.t, self.rb, self.o = t, rb, o

        def at(self, chunk, h):
            return chunk * 8 + h * 4 + first_of[h]

        def copies(self, stage, chunk):
            n = self.name
            if stage == 0:
                return [remote((n, 0, chunk), self.p.at[pl.ds(chunk * 8, 8), :, 1 - c], self.rc.at[pl.ds(chunk * 8, 8)], sibling)]
            if stage == 5:
                mine = self.o.at[pl.ds(chunk * 8, 8), :, c]
                return [remote((n, 5, chunk), mine, mine, sibling)]
            out = []
            for h in range(2):
                for i in range(1, 4):
                    key = (n, stage, chunk, h, i)
                    if stage in (1, 4):
                        a, peer = peer_first(h, i)
                    else:
                        b, peer = peer_second(h, i)
                    if stage == 1:
                        out.append(remote(key, self.q.at[chunk * 8 + h * 4 + a], self.ra.at[chunk, h, i - 1], peer))
                    elif stage == 2:
                        out.append(remote(key, self.t.at[chunk, h, b], self.rb.at[chunk, h, i - 1], peer))
                    elif stage == 3:
                        mine = self.o.at[self.at(chunk, h), second_of[h], c]
                        out.append(remote(key, mine, mine, peer))
                    else:
                        mine = self.o.at[self.at(chunk, h), :, c]
                        out.append(remote(key, mine, mine, peer))
            return out

        def after(self, stage, chunk):
            land(self.copies(stage, chunk))
            if stage == 0:
                part = pl.ds(chunk * 8, 8)
                self.q[part] = (self.p[part, :, c].astype(F32) + self.rc[part].astype(F32)).astype(BF16)
            elif stage == 1:
                for h in range(2):
                    total = self.q[self.at(chunk, h)].astype(F32)
                    for i in range(3):
                        total = total + self.ra[chunk, h, i].astype(F32)
                    self.t[chunk, h] = total.astype(BF16)
            elif stage == 2:
                for h in range(2):
                    total = self.t[chunk, h, second_of[h]].astype(F32)
                    for i in range(3):
                        total = total + self.rb[chunk, h, i].astype(F32)
                    self.o[self.at(chunk, h), second_of[h], c] = total.astype(BF16)
            elif stage == 5:
                mine = self.o

        def start(self, stage):
            go(self.copies(stage, 0))
            pl.when(wide)(lambda: go(self.copies(stage, 1)))

        def finish(self, stage):
            self.after(stage, 0)
            pl.when(wide)(lambda: self.after(stage, 1))

        def drain(self):
            for stage in range(6):
                sent(self.copies(stage, 0))
                pl.when(wide)(lambda: sent(self.copies(stage, 1)))

    class Scatter:
        def __init__(self, name, p, rc, q, ra, t, rb):
            self.name, self.p, self.rc, self.q = name, p, rc, q
            self.ra, self.t, self.rb = ra, t, rb

        def fill(self, left, right_ref):
            def chip(n, carry):
                cx, cy = n // 4, lax.rem(n, 4)
                columns = pl.ds(pl.multiple_of(n * 256, 256), 256)
                product = dot_nn(left, right_ref[:, columns]).astype(BF16)
                for core in range(2):
                    block = product[:, core * 128:(core + 1) * 128]
                    self.p[0, cx, cy, core] = block[:64]
                    self.p[1, cy, cx, core] = block[64:]
                return carry
            lax.fori_loop(0, 16, chip, 0)

        def copies(self, stage):
            n = self.name
            if stage == 0:
                return [remote((n, 0), self.p.at[:, :, :, 1 - c], self.rc, sibling)]
            out = []
            for h in range(2):
                for i in range(1, 4):
                    if stage == 1:
                        a, peer = peer_first(h, i)
                        out.append(remote((n, 1, h, i), self.q.at[h, a], self.ra.at[h, i - 1], peer))
                    else:
                        b, peer = peer_second(h, i)
                        out.append(remote((n, 2, h, i), self.t.at[h, b], self.rb.at[h, i - 1], peer))
            return out

        def start(self, stage):
            go(self.copies(stage))

        def finish(self, stage):
            land(self.copies(stage))
            if stage == 0:
                for h in range(2):
                    for a in range(4):
                        self.q[h, a] = (self.p[h, a, :, c].astype(F32) + self.rc[h, a].astype(F32)).astype(BF16)
            elif stage == 1:
                for h in range(2):
                    total = self.q[h, first_of[h]].astype(F32)
                    for i in range(3):
                        total = total + self.ra[h, i].astype(F32)
                    self.t[h] = total.astype(BF16)

        def result(self):
            halves = []
            for h in range(2):
                total = self.t[h, second_of[h]].astype(F32)
                for i in range(3):
                    total = total + self.rb[h, i].astype(F32)
                halves.append(total)
            return jnp.concatenate(halves, axis=0)

        def drain(self):
            for stage in range(3):
                sent(self.copies(stage))

    m_sum = Sum("m", m_p, m_rc, m_q, m_ra, m_t, m_rb, m_o)
    c_sum = Sum("c", c_p, c_rc, c_q, c_ra, c_t, c_rb, c_o)
    into = Scatter("i", i_p, i_rc, i_q, i_ra, i_t, i_rb)
    outof = Scatter("o", o_p, o_rc, o_q, o_ra, o_t, o_rb)

    @pl.when(s < last)
    def _():
        m_sum.start(0)
        m_sum.finish(0)
        m_sum.start(1)

    outof.fill(act_t[...], gl_ref)
    outof.start(0)

    @pl.when(s < last)
    def _():
        m_sum.finish(1)
        for stage in range(2, 6):
            m_sum.start(stage)
            m_sum.finish(stage)

    outof.finish(0)
    outof.start(1)

    @pl.when(s > 7)
    def _():
        go(roots_first())

    @pl.when(s <= 7)
    def _():
        roots_pack()

    def add_one(index):
        k = index - s - 1
        acc[...] += dot_nn(pg[index], m_o[k].reshape(128, 128))

    def cross(index):
        k = index - s - 1
        c_p[k] = dot_nn(act_t[...], pg[index]).astype(BF16).reshape(4, 2, 16, 128)

    def arrive(index):
        copy = pass_copy(index)
        copy.wait_recv()
        pl.when(s > 0)(lambda: copy.start())
        add_one(index)

    def link(n, carry):
        arrive(last - n)
        cross(last - n)
        return carry

    lax.fori_loop(0, last - s - 1, link, 0)

    @pl.when(s < last)
    def _():
        arrive(s + 1)
        pg[s] = (acc[...] * slope[...]).astype(BF16)
        pl.when(s > 0)(lambda: pass_copy(s).start())
        cross(s + 1)
        c_sum.start(0)

    into.fill(pg[s].astype(F32).T.astype(BF16), x_ref)
    into.start(0)
    outof.finish(1)
    outof.start(2)

    @pl.when(s < last)
    def _():
        c_sum.finish(0)
        c_sum.start(1)

    into.finish(0)
    into.start(1)

    @pl.when(s < last)
    def _():
        c_sum.finish(1)
        c_sum.start(2)
        c_sum.finish(2)
        c_sum.start(3)

    into.finish(1)
    into.start(2)

    @pl.when(s < last)
    def _():
        c_sum.finish(3)
        c_sum.start(4)

    @pl.when(s > 7)
    def _():
        roots_pack()

    land(roots_second())
    for h in range(2):
        total = r_pk[h, second_of[h]].astype(F32)
        for i in range(3):
            total = total + r_rk[h, i].astype(F32)
        r_sum[h] = total.astype(BF16)
    go(roots_pair())

    into.finish(2)
    land(roots_pair())
    for h in range(2):
        merged = (r_sum[h, c].astype(F32) + r_rc[h].astype(F32)).astype(BF16)
        for kind in range(2):
            for what in range(3):
                r_home[kind, what, pl.ds(h * 64, 64)] = merged[kind, what]

    def direct(kind, grad32, out_ref):
        grad = grad32.astype(BF16)
        exact = grad.astype(F32)
        first = dot_nn(r_home[kind, 0], grad)
        high = first.astype(BF16)
        low = (first - high.astype(F32)).astype(BF16)
        right = r_home[kind, 1]
        precond = dot_nn(high, right) + dot_nn(low, right)
        grad_sq = jnp.sum(jnp.sum(exact * exact, axis=1, keepdims=True), axis=0, keepdims=True)
        pre_sq = jnp.sum(jnp.sum(precond * precond, axis=1, keepdims=True), axis=0, keepdims=True)
        direction = precond * (jnp.sqrt(grad_sq) * lax.rsqrt(pre_sq + 1e-06))
        out_ref[...] = (MOMENTUM_DECAY * r_home[kind, 2].astype(F32) + direction).astype(BF16)
        rounded = direction.astype(BF16)
        for h in range(2):
            d_x[h, first_of[h], c, kind] = rounded[h * 64:(h + 1) * 64]

    direct(0, into.result().T * (1.0 / 32), search_in_ref)

    outof.finish(2)
    acc[...] = outof.result()

    @pl.when(s < last)
    def _():
        c_sum.finish(4)
        c_sum.start(5)
        c_sum.finish(5)

        def term(k, carry):
            acc[...] += dot_nt(c_o[k].reshape(128, 128), wz[s + 1 + k])
            return carry
        lax.fori_loop(0, last - s, term, 0)

    direct(1, acc[...] * (1.0 / 32), search_out_ref)

    def way_first():
        copies = []
        for h in range(2):
            mine = d_x.at[h, first_of[h], c]
            for i in range(1, 4):
                copies.append(remote(("da", h, i), mine, mine, peer_first(h, i)[1]))
        return copies

    def way_pair():
        mine = d_x.at[:, :, c]
        return [remote(("dc",), mine, mine, sibling)]

    def way_second():
        copies = []
        for h in range(2):
            for i in range(1, 4):
                b, peer = peer_second(h, i)
                copies.append(remote(("db", h, i), d_pk.at[h, b], d_rk.at[h, i - 1], peer))
        return copies

    go(way_first())
    land(way_first())
    go(way_pair())
    land(way_pair())
    for h in range(2):
        def slot(t, carry):
            b, k = t // 4, lax.rem(t, 4)
            owner = device(h, first_of[h], b)
            block = lists[owner * 4 + k]
            kind = block // 32
            hx, hy, core = lax.rem(block // 8, 4), lax.rem(block // 2, 4), lax.rem(block, 2)
            a, row = (hx, hy) if h == 0 else (hy, hx)
            here = (row == second_of[h]) & (count[owner] > k)
            value = d_x[h, a, core, kind]
            d_pk[h, b, k] = jnp.where(here, value, jnp.zeros_like(value))
            return carry
        lax.fori_loop(0, 16, slot, 0)
    go(way_second())
    land(way_second())
    for h in range(2):
        total = d_pk[h, second_of[h]].astype(F32)
        for i in range(3):
            total = total + d_rk[h, i].astype(F32)
        rows = pl.ds(h * 64, 64)
        for k in range(4):
            old = mom_ref[k, rows]
            new = MOMENTUM_DECAY * old + total[k]
            newmom_ref[k, rows] = jnp.where(count[dp] > k, new, old)

    @pl.when(s > 0)
    def _():
        def leave(n, carry):
            slice_copy(s + n).wait_send()
            pass_copy(s + n).wait_send()
            return carry
        lax.fori_loop(0, sections - s, leave, 0)

    @pl.when(s < last)
    def _():
        m_sum.drain()
        c_sum.drain()
    into.drain()
    outof.drain()
    sent(roots_first())
    sent(roots_second())
    sent(roots_pair())
    sent(way_first())
    sent(way_pair())
    sent(way_second())


def on_device(
    sections, saved_inputs, loss_grad, w_in, w_out, left_root, right_root, momentum, owned_blocks, owned_count
):
    vmem = pl.BlockSpec(memory_space=pltpu.VMEM)
    smem = pl.BlockSpec(memory_space=pltpu.SMEM)

    def room(*shape, kind=BF16):
        return pltpu.VMEM(shape, kind)

    def sum_room():
        return [
            room(16, 4, 2, 16, 128), room(16, 4, 16, 128), room(16, 4, 16, 128),
            room(2, 2, 3, 4, 16, 128), room(2, 2, 4, 16, 128), room(2, 2, 3, 16, 128),
            room(16, 4, 2, 16, 128),
        ]

    def scatter_room():
        return [
            room(2, 4, 4, 2, 64, 128), room(2, 4, 4, 64, 128), room(2, 4, 4, 64, 128),
            room(2, 3, 4, 64, 128), room(2, 4, 64, 128), room(2, 3, 64, 128),
        ]

    scratch = (
        [room(sections, 128, 128), room(sections, 128, 128), room(128, 128, kind=F32), room(128, 128, kind=F32), room(128, 128)]
        + sum_room() + sum_room() + scatter_room() + scatter_room()
        + [
            room(2, 16, 3, 64, 128), room(2, 4, 2, 2, 3, 64, 128), room(2, 3, 2, 2, 3, 64, 128),
            room(2, 2, 2, 3, 64, 128), room(2, 2, 3, 64, 128), room(2, 3, 128, 128),
            room(2, 4, 2, 2, 64, 128), room(2, 4, 4, 64, 128), room(2, 3, 4, 64, 128),
        ]
        + [pltpu.SemaphoreType.DMA((COPIES,))] * 2
        + [pltpu.SemaphoreType.DMA((sections,))] * 4
    )
    new_mom, search_in, search_out = pl.pallas_call(
        functools.partial(kernel, sections),
        out_shape=(
            jax.ShapeDtypeStruct((4, 128, 128), F32),
            jax.ShapeDtypeStruct((128, 128), BF16),
            jax.ShapeDtypeStruct((128, 128), BF16),
        ),
        in_specs=[vmem] * 7 + [smem] * 2,
        out_specs=(vmem, vmem, vmem),
        scratch_shapes=scratch,
        compiler_params=pltpu.CompilerParams(
            collective_id=0, has_side_effects=True, vmem_limit_bytes=48 * 1024 * 1024
        ),
        name="drain",
    )(
        saved_inputs.reshape(128, 4096), loss_grad.reshape(128, 4096), w_in[0], w_out[0],
        left_root[0, 0], right_root[0, 0], momentum[0, 0],
        owned_blocks.reshape(128), owned_count.reshape(32),
    )
    return new_mom[None, None], search_in[None], search_out[None]


def solution(mesh):
    placed = (
        P("section", None, "dp", None),
        P(None, "dp", None),
        P("section", None, None),
        P("section", None, None),
        P("section", "dp", None, None, None),
        P("section", "dp", None, None, None),
        P("section", "dp", None, None, None),
        P("section", None, None),
        P("section", None),
    )
    return jax.shard_map(
        functools.partial(on_device, mesh.shape["section"]),
        mesh=mesh,
        in_specs=placed,
        out_specs=(
            P("section", "dp", None, None, None),
            P("section", "dp", None),
            P("section", None, "dp"),
        ),
        check_vma=False,
    )
```

time: 446 us -> 136 us (0.30); the launches traced: 441 us -> 136 us
  waiting for transfers between devices: 246 us -> 0 us
  Pallas kernels: 0 us -> 124 us
  starting transfers between devices: 46.9 us -> 0 us
  matrix products: 45.2 us -> 0 us
  blocking collectives: 35.1 us -> 0 us
  other arithmetic: 29.3 us -> 0 us
  local copies, waits for them, and re-layouts: 35.8 us -> 11 us
    ppermute x17 -> x0, waiting for transfers between devices: 194 us -> none  [passed_along(): lax.ppermute(value, axis, [(source, source + steps) for source in range(i...]
    pallas_call x0 -> x1, Pallas kernels: none -> 124 us  [on_device(): pl.pallas_call(functools.partial(kernel, sections), out_shape=(jax.ShapeD...]
    all_to_all x1 -> x0, waiting for transfers between devices: 51.7 us -> none  [on_device(): lax.all_to_all(outgoing, 'dp', split_axis=0, concat_axis=0, tiled=True)]
    dot_general x58 -> x0, matrix products: 45.2 us -> none  [the longest x34 29.9 us: contract_cols(): lax.dot_general(left_side, right_side, (((1,), (1,)), ((), ())), preferre...]
    all_to_all x1 -> x0, blocking collectives: 35.1 us -> none  [on_device(): lax.all_to_all(packed, 'dp', split_axis=0, concat_axis=0, tiled=True)]
    all_to_all x1 -> x0, starting transfers between devices: 25.2 us -> none  [on_device(): lax.all_to_all(outgoing, 'dp', split_axis=0, concat_axis=0, tiled=True)]
    select_n x19 -> x0, other arithmetic: 22.7 us -> none  [the longest x17 18.8 us: tick(): upper = jnp.where(section_index == section_count - 1, given, incoming)]
    ppermute x17 -> x0, starting transfers between devices: 21.8 us -> none  [passed_along(): lax.ppermute(value, axis, [(source, source + steps) for source in range(i...]
  transfers between devices with their start and end apart: 18 -> 0, of which waited for: 18 -> 0; matrix products, arithmetic and copies ran while one was open for 2% -> 0% of each run, Pallas kernels for 0% -> 0%
where the time goes in v1:
time: 136 us
  Pallas kernels  124 us (91%)
  local copies, waits for them, and re-layouts  11 us (8%)
    pallas_call x1, Pallas kernels, on_device(): pl.pallas_call(functools.partial(kernel, sections), out_shape=(jax.ShapeD...  124 us
    unnamed x22, local copies, waits for them, and re-layouts  10.9 us

profile of v1, /device:TPU:1, one launch (start us, length us, event | category | flops | bytes accessed | tf_op | source)
XLA Modules:
  0.0 136.0 jit_solution(3477165996197467387)
XLA Ops:
  0.6 0.0 copy-start.8
  0.6 0.7 copy-done.8
  1.3 0.1 copy.13
  1.4 0.0 copy-start.7
  1.4 0.1 reshape.20.lists
  1.5 0.5 copy-done.7
  2.1 0.0 copy-start
  2.1 1.2 copy-done
  3.3 0.0 copy-start.1
  3.3 1.2 copy-done.1
  4.5 0.0 copy-start.2
  4.5 1.2 copy-done.2
  5.7 0.0 copy-start.3
  5.7 1.2 copy-done.3
  7.0 0.0 copy-start.4
  7.0 0.9 copy-done.4
  7.9 0.0 copy-start.5
  7.9 0.9 copy-done.5
  8.8 0.0 copy-start.6
  8.8 0.9 copy-done.6
  9.7 124.4 %drain.1 = (f32[4,128,128]{2,1,0:T(8,128)S(1)}, bf16[128,128]{1,0:T(8,128)(2,1)S(1)}, bf16[128,128]{1,0:T(8,128)(2,1)S(1)}) custom-call(bf16[128,4096]{1,0:T(8,128)(2,1)S(1)} %bitcast.11, bf16[128,4096]{1,0:T(8,128)(2,1)S(1)} %bitcast.12, bf16[4096,128]{1,0:T(8,128)(2,1)S(1)} %bitcast.13, bf16[128,4096]{1,0:T(8,128)(2,1)S(1)} %bitcast.14, ...), custom_call_target="tpu_custom_call" | custom-call | tf_op jit(solution)/shard_map/drain/pallas_call | solution.py:578
  134.1 0.7 copy.17
  134.8 0.6 copy.18
  135.4 0.6 copy.19
Async XLA Ops:
  0.6 0.7 copy-start.8
  1.4 0.7 copy-start.7
  2.1 1.2 copy-start
  3.3 1.2 copy-start.1
  4.5 1.2 copy-start.2
  5.7 1.2 copy-start.3
  7.0 0.9 copy-start.4
  7.9 0.9 copy-start.5
  8.8 0.9 copy-start.6

commit v2 on v1

v2 whole, which is shorter than its diff:
```python
import functools

import jax
import jax.numpy as jnp
from jax import lax
from jax.experimental import pallas as pl
from jax.experimental.pallas import tpu as pltpu
from jax.sharding import PartitionSpec as P

MOMENTUM_DECAY = 0.9
MESH = pl.DeviceIdType.MESH
BF16 = jnp.bfloat16
F32 = jnp.float32
COPIES = 72
EARLY = 3
SOON = 8


def dot_nn(a, b):
    return lax.dot_general(a, b, (((1,), (0,)), ((), ())), preferred_element_type=F32)


def dot_nt(a, b):
    return lax.dot_general(a, b, (((1,), (1,)), ((), ())), preferred_element_type=F32)


def silu_slope(values):
    sigma = jax.nn.sigmoid(values)
    return sigma * (1.0 + values * (1.0 - sigma))


def kernel(
    sections,
    x_hbm, gl_hbm, win_hbm, wout_hbm, left_hbm, right_hbm, mom_hbm, lists_ref, count_ref,
    newmom_ref, search_in_ref, search_out_ref,
    x_ref, gl_ref, win_ref, wout_ref, mom_ref,
    wz, pg, slope, base, acc, acc_out, act_t, slope_next, acc_next, m_next,
    m_p, m_rc, m_o,
    c_p, c_rc, c_o,
    i_p, i_rc, i_q, i_ra, i_t, i_rb,
    o_p, o_rc, o_q, o_ra, o_t, o_rb,
    r_x, r_pk, r_rk, r_sum, r_rc, r_home,
    d_x, d_pk, d_rk,
    local, send, recv, z_near, z_far, z_recv, p_near, p_far, p_recv, n_send, n_recv, b_send, b_recv,
):
    s = lax.axis_index("section")
    dp = lax.axis_index("dp")
    c = lax.rem(dp, 2)
    y = lax.rem(dp // 2, 4)
    x = dp // 8
    last = sections - 1
    first_of = (x, y)
    second_of = (y, x)
    wide = s <= last - 9
    ids = {}

    def sid(key):
        return ids.setdefault(key, len(ids))

    def device(h, a, b):
        return (a * 4 + b) * 2 + c if h == 0 else (b * 4 + a) * 2 + c

    def remote(key, source, target, peer):
        number = sid(key)
        return pltpu.make_async_remote_copy(
            src_ref=source, dst_ref=target, send_sem=send.at[number], recv_sem=recv.at[number],
            device_id={"dp": peer}, device_id_type=MESH,
        )

    sibling = dp + 1 - 2 * c

    def peer_first(h, i):
        a = lax.rem(first_of[h] + i, 4)
        return a, device(h, a, second_of[h])

    def peer_second(h, i):
        b = lax.rem(second_of[h] + i, 4)
        return b, device(h, first_of[h], b)

    def go(copies):
        for copy in copies:
            copy.start()

    def land(copies):
        for copy in copies:
            copy.wait_recv()

    def sent(copies):
        for copy in copies:
            copy.wait_send()

    barrier = pltpu.get_barrier_semaphore()

    def greet(i, carry):
        pl.semaphore_signal(barrier, inc=1, device_id={"dp": lax.rem(dp + i, 32)}, device_id_type=MESH)
        return carry

    lax.fori_loop(1, 32, greet, 0)
    below = lax.rem(s + last, sections)
    below_two = lax.rem(s + last - 1, sections)
    even = lax.rem(s, 2) == 0
    for peer in (below, below_two, lax.rem(s + 1, sections), lax.rem(s + 2, sections)):
        pl.semaphore_signal(barrier, inc=1, device_id={"section": peer}, device_id_type=MESH)

    fetches = {}

    def fetch(name, source, target):
        fetches[name] = pltpu.make_async_copy(source, target, local.at[len(fetches)])
        fetches[name].start()

    fetch("x", x_hbm, x_ref)
    fetch("win", win_hbm, win_ref)
    fetch("gl", gl_hbm, gl_ref)
    fetch("wout", wout_hbm, wout_ref)
    fetch("mom", mom_hbm, mom_ref)
    for h in range(2):
        rows = pl.ds(h * 64, 64)
        slots = pl.ds(first_of[h] * 4, 4)
        fetch(("left", h), left_hbm.at[:, rows], r_x.at[h, slots, 0])
        fetch(("right", h), right_hbm.at[:, rows], r_x.at[h, slots, 1])

    pl.semaphore_wait(barrier, 35)

    def to_section(source, target, send_sem, recv_sem, peer):
        return pltpu.make_async_remote_copy(
            src_ref=source, dst_ref=target, send_sem=send_sem, recv_sem=recv_sem,
            device_id={"section": peer}, device_id_type=MESH,
        )

    def slice_near(index):
        return to_section(wz.at[index], wz.at[index], z_near.at[index], z_recv.at[index], below)

    def slice_far(index):
        return to_section(wz.at[index], wz.at[index], z_far.at[index], z_recv.at[index], below_two)

    my_columns = pl.ds(pl.multiple_of(dp * 128, 128), 128)

    def own_near():
        return to_section(win_hbm.at[my_columns], wz.at[s], z_near.at[s], z_recv.at[s], below)

    def own_far():
        return to_section(win_hbm.at[my_columns], wz.at[s], z_far.at[s], z_recv.at[s], below_two)

    def pass_near(index):
        return to_section(pg.at[index], pg.at[index], p_near.at[index], p_recv.at[index], below)

    def pass_far(index):
        return to_section(pg.at[index], pg.at[index], p_far.at[index], p_recv.at[index], below_two)

    def share_state():
        return [
            to_section(base, acc_next, b_send.at[0], b_recv.at[0], below),
            to_section(slope, slope_next, b_send.at[1], b_recv.at[1], below),
        ]

    def places(k):
        if isinstance(k, int):
            return k // 8, k // 4 % 2, k % 4
        return k // 8, lax.rem(k // 4, 2), lax.rem(k, 4)

    def share_product(k):
        return to_section(m_o.at[places(k)], m_next.at[k], n_send.at[k], n_recv.at[k], below)

    pl.when(s > 1)(lambda: own_far().start())
    pl.when(s > 0)(lambda: own_near().start())

    def roots_first():
        copies = []
        for h in range(2):
            mine = r_x.at[h, pl.ds(first_of[h] * 4, 4)]
            for i in range(1, 4):
                copies.append(remote(("ra", h, i), mine, mine, peer_first(h, i)[1]))
        return copies

    def roots_second():
        copies = []
        for h in range(2):
            for i in range(1, 4):
                b, peer = peer_second(h, i)
                copies.append(remote(("rb", h, i), r_pk.at[h, b], r_rk.at[h, i - 1], peer))
        return copies

    def roots_pair():
        return [remote(("rc",), r_sum.at[:, 1 - c], r_rc, sibling)]

    def roots_pack():
        land(roots_first())
        for h in range(2):
            def target(t, carry):
                b, core, kind = t // 4, lax.rem(t // 2, 2), lax.rem(t, 2)
                if h == 0:
                    place = (first_of[h] * 4 + b) * 2 + core
                else:
                    place = (b * 4 + first_of[h]) * 2 + core
                block = kind * 32 + place
                index = jnp.int32(0)
                found = jnp.int32(0)
                for a in range(4):
                    owner = device(h, a, second_of[h])
                    held = count_ref[0, owner]
                    for k in range(4):
                        hit = (lists_ref[0, k, owner] == block) & (held > k)
                        index = index + jnp.where(hit, a * 4 + k, 0)
                        found = found + jnp.where(hit, 1, 0)
                value = r_x[h, index]
                r_pk[h, b, core, kind] = jnp.where(found > 0, value, jnp.zeros_like(value))
                return carry
            lax.fori_loop(0, 16, target, 0)
        go(roots_second())

    fetches["x"].wait()
    fetches["win"].wait()
    pre = dot_nn(x_ref[...], win_ref[...])
    slope[...] = silu_slope(pre)
    act = jax.nn.silu(pre)
    act_t[...] = act.T.astype(BF16)
    fetches["gl"].wait()
    fetches["wout"].wait()
    base[...] = dot_nt(gl_ref[...], wout_ref[...])
    acc[...] = base[...]

    @pl.when(~even)
    def _():
        go(share_state())

    fetches["mom"].wait()
    for h in range(2):
        for k in range(4):
            r_x[h, first_of[h] * 4 + k, 2] = mom_ref[k, pl.ds(h * 64, 64)].astype(BF16)
        fetches[("left", h)].wait()
        fetches[("right", h)].wait()

    @pl.when(s <= SOON)
    def _():
        go(roots_first())

    wz[sections:] = jnp.zeros_like(wz[sections:])
    m_p[...] = jnp.zeros_like(m_p)
    c_p[...] = jnp.zeros_like(c_p)

    class Sum:
        def __init__(self, name, p, rc, o):
            self.name, self.p, self.rc, self.o = name, p, rc, o

        def start(self, stage, first, size):
            number = sid((self.name, stage, first))
            part = pl.ds(first, size)

            def one(i, carry):
                peer = lax.rem(dp + i, 32)
                if stage == 0:
                    source = self.p.at[part, :, peer // 8, lax.rem(peer // 2, 4), lax.rem(peer, 2)]
                    target = self.rc.at[i - 1, part]
                else:
                    source = target = self.o.at[part, :, x, y, c]
                pltpu.make_async_remote_copy(
                    src_ref=source, dst_ref=target, send_sem=send.at[number], recv_sem=recv.at[number],
                    device_id={"dp": peer}, device_id_type=MESH,
                ).start()
                return carry

            lax.fori_loop(1, 32, one, 0)

        def all_bytes(self, sems, stage, first, size):
            number = sid((self.name, stage, first))
            every = self.rc.at[:, pl.ds(first, size)]
            pltpu.make_async_copy(every, every, sems.at[number]).wait()

        def finish(self, stage, first, size):
            self.all_bytes(recv, stage, first, size)
            if stage == 0:
                part = pl.ds(first, size)
                total = self.p[part, :, x, y, c].astype(F32)
                for i in range(31):
                    total = total + self.rc[i, part].astype(F32)
                self.o[part, :, x, y, c] = total.astype(BF16)

        def drain(self, first, size):
            for stage in range(2):
                self.all_bytes(send, stage, first, size)

    class Scatter:
        def __init__(self, name, p, rc, q, ra, t, rb):
            self.name, self.p, self.rc, self.q = name, p, rc, q
            self.ra, self.t, self.rb = ra, t, rb

        def fill(self, left, right_ref):
            def chip(n, carry):
                cx, cy = n // 4, lax.rem(n, 4)
                columns = pl.ds(pl.multiple_of(n * 256, 256), 256)
                product = dot_nn(left, right_ref[:, columns]).astype(BF16)
                for core in range(2):
                    block = product[:, core * 128:(core + 1) * 128]
                    self.p[0, cx, cy, core] = block[:64]
                    self.p[1, cy, cx, core] = block[64:]
                return carry
            lax.fori_loop(0, 16, chip, 0)

        def copies(self, stage):
            n = self.name
            if stage == 0:
                return [remote((n, 0), self.p.at[:, :, :, 1 - c], self.rc, sibling)]
            out = []
            for h in range(2):
                for i in range(1, 4):
                    if stage == 1:
                        a, peer = peer_first(h, i)
                        out.append(remote((n, 1, h, i), self.q.at[h, a], self.ra.at[h, i - 1], peer))
                    else:
                        b, peer = peer_second(h, i)
                        out.append(remote((n, 2, h, i), self.t.at[h, b], self.rb.at[h, i - 1], peer))
            return out

        def start(self, stage):
            go(self.copies(stage))

        def finish(self, stage):
            land(self.copies(stage))
            if stage == 0:
                for h in range(2):
                    for a in range(4):
                        self.q[h, a] = (self.p[h, a, :, c].astype(F32) + self.rc[h, a].astype(F32)).astype(BF16)
            elif stage == 1:
                for h in range(2):
                    total = self.q[h, first_of[h]].astype(F32)
                    for i in range(3):
                        total = total + self.ra[h, i].astype(F32)
                    self.t[h] = total.astype(BF16)

        def result(self):
            halves = []
            for h in range(2):
                total = self.t[h, second_of[h]].astype(F32)
                for i in range(3):
                    total = total + self.rb[h, i].astype(F32)
                halves.append(total)
            return jnp.concatenate(halves, axis=0)

        def drain(self):
            for stage in range(3):
                sent(self.copies(stage))

    m_sum = Sum("m", m_p, m_rc, m_o)
    c_sum = Sum("c", c_p, c_rc, c_o)
    into = Scatter("i", i_p, i_rc, i_q, i_ra, i_t, i_rb)
    outof = Scatter("o", o_p, o_rc, o_q, o_ra, o_t, o_rb)

    def product(t):
        block = dot_nn(wout_ref[:, my_columns], wz[s + t])
        m_p[places(t - 1)] = block.astype(BF16).reshape(4, 2, 16, 128)

    def relay(n, carry):
        odd = 2 * n + 1
        far = 2 * n + 2
        slice_far(s + far).wait_recv()

        @pl.when(s > 1)
        def _():
            slice_far(s + far).start()
            slice_near(s + far).start()

        pl.when(s == 1)(lambda: slice_near(s + far).start())
        slice_near(s + odd).wait_recv()
        product(odd)
        product(far)

        @pl.when(wide & (n == 3))
        def _():
            m_sum.start(0, 0, 1)

        @pl.when(wide & (n == 4))
        def _():
            m_sum.finish(0, 0, 1)
            m_sum.start(1, 0, 1)

        @pl.when(wide & (n == 5))
        def _():
            m_sum.finish(1, 0, 1)
        return carry

    steps = (last - s) // 2
    lax.fori_loop(0, steps, relay, 0)

    @pl.when(even)
    def _():
        slice_near(last).wait_recv()
        product(last - s)

    @pl.when(wide)
    def _():
        @pl.when(steps < 5)
        def _():
            m_sum.finish(0, 0, 1)
            m_sum.start(1, 0, 1)

        m_sum.start(0, 1, 1)
        pl.when(steps < 6)(lambda: m_sum.finish(1, 0, 1))

    pl.when((~wide) & (s < last))(lambda: m_sum.start(0, 0, 1))

    @pl.when(s <= EARLY)
    def _():
        outof.fill(act_t[...], gl_ref)
        outof.start(0)

    @pl.when(wide)
    def _():
        m_sum.finish(0, 1, 1)
        m_sum.start(1, 1, 1)

    @pl.when(s <= EARLY)
    def _():
        outof.finish(0)
        roots_pack()
        outof.start(1)

    pl.when(wide)(lambda: m_sum.finish(1, 1, 1))

    @pl.when((~wide) & (s < last))
    def _():
        m_sum.finish(0, 0, 1)
        m_sum.start(1, 0, 1)
        m_sum.finish(1, 0, 1)

    @pl.when(~even)
    def _():
        def give(k, carry):
            share_product(k).start()
            return carry
        lax.fori_loop(0, last - s, give, 0)

    pl.when(s > SOON)(lambda: go(roots_first()))

    def cross(index):
        c_p[places(index - s - 1)] = dot_nn(act_t[...], pg[index]).astype(BF16).reshape(4, 2, 16, 128)

    def own_term(index):
        return dot_nt(pg[index], m_o[places(index - s - 1)].reshape(128, 128))

    def next_term(index):
        return dot_nt(pg[index], m_next[index - s - 2].reshape(128, 128))

    lowest = (s + 2) // 2

    @pl.when(even)
    def _():
        land(share_state())

        def come(high, low):
            pass_far(high).wait_recv()
            pass_far(low).wait_recv()

            @pl.when(s > 0)
            def _():
                pass_far(high).start()
                pass_far(low).start()

        def products(high, low):
            share_product(high - s - 2).wait_recv()
            share_product(low - s - 2).wait_recv()

        def collect(n, carry):
            high, low = 15 - 2 * n, 14 - 2 * n
            come(high, low)

            @pl.when(s > 0)
            def _():
                pass_near(high).start()
                pass_near(low).start()
            return carry

        def add(n, carry):
            high, low = 15 - 2 * n, 14 - 2 * n
            products(high, low)
            acc_next[...] += next_term(high) + next_term(low)
            acc[...] += own_term(high) + own_term(low)
            return carry

        lax.fori_loop(0, 7 - lowest, collect, 0)
        lax.fori_loop(0, 7 - lowest, add, 0)

        @pl.when(s < last - 1)
        def _():
            high, low = 2 * lowest + 1, 2 * lowest
            products(high, low)
            come(high, low)
            pg[s + 1] = ((acc_next[...] + next_term(high) + next_term(low)) * slope_next[...]).astype(BF16)
            pl.when(s > 0)(lambda: pass_far(s + 1).start())
            pg[s] = ((acc[...] + own_term(high) + own_term(low) + own_term(s + 1)) * slope[...]).astype(BF16)

            @pl.when(s > 0)
            def _():
                pass_far(s).start()
                for index in (high, low, s + 1, s):
                    pass_near(index).start()

        @pl.when(s == last - 1)
        def _():
            pg[s + 1] = (acc_next[...] * slope_next[...]).astype(BF16)
            pass_far(s + 1).start()
            pg[s] = ((acc[...] + own_term(s + 1)) * slope[...]).astype(BF16)
            pass_far(s).start()
            pass_near(s + 1).start()
            pass_near(s).start()

    @pl.when(~even)
    def _():
        def collect(n, carry):
            high, low = 15 - 2 * n, 14 - 2 * n
            pass_far(high).wait_recv()
            pass_far(low).wait_recv()
            acc[...] += own_term(high) + own_term(low)
            return carry

        lax.fori_loop(0, 8 - lowest, collect, 0)
        pg[s] = (acc[...] * slope[...]).astype(BF16)

    def cross_two(n, carry):
        cross(s + 1 + 2 * n)
        cross(s + 2 + 2 * n)
        return carry

    lax.fori_loop(0, (last - s) // 2, cross_two, 0)
    pl.when(even)(lambda: cross(last))
    pl.when(wide)(lambda: c_sum.start(0, 0, 2))
    pl.when((~wide) & (s < last))(lambda: c_sum.start(0, 0, 1))

    into.fill(pg[s].astype(F32).T.astype(BF16), x_ref)
    into.start(0)

    into.finish(0)
    into.start(1)

    @pl.when(wide)
    def _():
        c_sum.finish(0, 0, 2)
        c_sum.start(1, 0, 2)

    @pl.when((~wide) & (s < last))
    def _():
        c_sum.finish(0, 0, 1)
        c_sum.start(1, 0, 1)

    @pl.when(s > EARLY)
    def _():
        roots_pack()
        outof.fill(act_t[...], gl_ref)
        outof.start(0)
        outof.finish(0)
        outof.start(1)

    outof.finish(1)
    outof.start(2)
    into.finish(1)
    into.start(2)

    land(roots_second())
    for h in range(2):
        total = r_pk[h, second_of[h]].astype(F32)
        for i in range(3):
            total = total + r_rk[h, i].astype(F32)
        r_sum[h] = total.astype(BF16)
    go(roots_pair())

    def terms(first):
        total = acc_out[...]
        for k in range(first, first + 8):
            total = total + dot_nt(c_o[places(k)].reshape(128, 128), wz[s + 1 + k])
        acc_out[...] = total

    outof.finish(2)
    acc_out[...] = outof.result()

    into.finish(2)
    land(roots_pair())
    for h in range(2):
        merged = (r_sum[h, c].astype(F32) + r_rc[h].astype(F32)).astype(BF16)
        for kind in range(2):
            for what in range(3):
                r_home[kind, what, pl.ds(h * 64, 64)] = merged[kind, what]

    def direct(kind, grad32, out_ref):
        grad = grad32.astype(BF16)
        exact = grad.astype(F32)
        first = dot_nn(r_home[kind, 0], grad)
        high = first.astype(BF16)
        low = (first - high.astype(F32)).astype(BF16)
        right = r_home[kind, 1]
        precond = dot_nn(high, right) + dot_nn(low, right)
        grad_sq = jnp.sum(jnp.sum(exact * exact, axis=1, keepdims=True), axis=0, keepdims=True)
        pre_sq = jnp.sum(jnp.sum(precond * precond, axis=1, keepdims=True), axis=0, keepdims=True)
        direction = precond * (jnp.sqrt(grad_sq) * lax.rsqrt(pre_sq + 1e-06))
        out_ref[...] = (MOMENTUM_DECAY * r_home[kind, 2].astype(F32) + direction).astype(BF16)
        rounded = direction.astype(BF16)
        for h in range(2):
            d_x[h, first_of[h], c, kind] = rounded[h * 64:(h + 1) * 64]

    direct(0, into.result().T * (1.0 / 32), search_in_ref)

    def way_first(kind):
        copies = []
        for h in range(2):
            mine = d_x.at[h, first_of[h], c, kind]
            for i in range(1, 4):
                copies.append(remote(("da", h, i, kind), mine, mine, peer_first(h, i)[1]))
        return copies

    go(way_first(0))

    @pl.when(wide)
    def _():
        c_sum.finish(1, 0, 2)
        terms(8)
        terms(0)

    @pl.when((~wide) & (s < last))
    def _():
        c_sum.finish(1, 0, 1)
        terms(0)

    direct(1, acc_out[...] * (1.0 / 32), search_out_ref)

    def way_pair():
        mine = d_x.at[:, :, c]
        return [remote(("dc",), mine, mine, sibling)]

    def way_second():
        copies = []
        for h in range(2):
            for i in range(1, 4):
                b, peer = peer_second(h, i)
                copies.append(remote(("db", h, i), d_pk.at[h, b], d_rk.at[h, i - 1], peer))
        return copies

    go(way_first(1))
    land(way_first(0))
    land(way_first(1))
    go(way_pair())
    land(way_pair())
    for h in range(2):
        def slot(t, carry):
            b, k = t // 4, lax.rem(t, 4)
            owner = device(h, first_of[h], b)
            block = lists_ref[0, k, owner]
            kind = block // 32
            hx, hy, core = lax.rem(block // 8, 4), lax.rem(block // 2, 4), lax.rem(block, 2)
            a, row = (hx, hy) if h == 0 else (hy, hx)
            here = (row == second_of[h]) & (count_ref[0, owner] > k)
            value = d_x[h, a, core, kind]
            d_pk[h, b, k] = jnp.where(here, value, jnp.zeros_like(value))
            return carry
        lax.fori_loop(0, 16, slot, 0)
    go(way_second())
    land(way_second())
    for h in range(2):
        total = d_pk[h, second_of[h]].astype(F32)
        for i in range(3):
            total = total + d_rk[h, i].astype(F32)
        rows = pl.ds(h * 64, 64)
        for k in range(4):
            old = mom_ref[k, rows]
            new = MOMENTUM_DECAY * old + total[k]
            newmom_ref[k, rows] = jnp.where(count_ref[0, dp] > k, new, old)

    pl.when(s > 1)(lambda: own_far().wait_send())
    pl.when(s > 0)(lambda: own_near().wait_send())

    def leave(t, carry):
        @pl.when(lax.rem(t, 2) == 0)
        def _():
            pl.when(s > 1)(lambda: slice_far(s + t).wait_send())
            pl.when(s > 0)(lambda: slice_near(s + t).wait_send())
        return carry

    lax.fori_loop(1, sections - s, leave, 0)

    @pl.when(even & (s > 0))
    def _():
        def passed(index, carry):
            pass_far(index).wait_send()
            pass_near(index).wait_send()
            return carry
        lax.fori_loop(s, sections, passed, 0)

    @pl.when(~even)
    def _():
        sent(share_state())

        def given(k, carry):
            share_product(k).wait_send()
            return carry
        lax.fori_loop(0, last - s, given, 0)

    @pl.when(wide)
    def _():
        m_sum.drain(0, 1)
        m_sum.drain(1, 1)
        c_sum.drain(0, 2)

    @pl.when((~wide) & (s < last))
    def _():
        m_sum.drain(0, 1)
        c_sum.drain(0, 1)

    into.drain()
    outof.drain()
    sent(roots_first())
    sent(roots_second())
    sent(roots_pair())
    sent(way_first(0))
    sent(way_first(1))
    sent(way_pair())
    sent(way_second())


def on_device(
    sections, saved_inputs, loss_grad, w_in, w_out, left_root, right_root, momentum, owned_blocks, owned_count
):
    vmem = pl.BlockSpec(memory_space=pltpu.VMEM)
    hbm = pl.BlockSpec(memory_space=pltpu.HBM)
    smem = pl.BlockSpec(memory_space=pltpu.SMEM)

    def room(*shape, kind=BF16):
        return pltpu.VMEM(shape, kind)

    def sum_room():
        return [
            room(2, 2, 4, 4, 2, 16, 128), room(31, 2, 2, 16, 128), room(2, 2, 4, 4, 2, 16, 128),
        ]

    def scatter_room():
        return [
            room(2, 4, 4, 2, 64, 128), room(2, 4, 4, 64, 128), room(2, 4, 4, 64, 128),
            room(2, 3, 4, 64, 128), room(2, 4, 64, 128), room(2, 3, 64, 128),
        ]

    scratch = (
        [
            room(128, 4096), room(128, 4096), room(4096, 128), room(128, 4096), room(4, 128, 128, kind=F32),
            room(sections + 8, 128, 128), room(sections, 128, 128),
            room(128, 128, kind=F32), room(128, 128, kind=F32), room(128, 128, kind=F32), room(128, 128, kind=F32), room(128, 128),
            room(128, 128, kind=F32), room(128, 128, kind=F32), room(16, 4, 2, 16, 128),
        ]
        + sum_room() + sum_room() + scatter_room() + scatter_room()
        + [
            room(2, 16, 3, 64, 128), room(2, 4, 2, 2, 3, 64, 128), room(2, 3, 2, 2, 3, 64, 128),
            room(2, 2, 2, 3, 64, 128), room(2, 2, 3, 64, 128), room(2, 3, 128, 128),
            room(2, 4, 2, 2, 64, 128), room(2, 4, 4, 64, 128), room(2, 3, 4, 64, 128),
        ]
        + [pltpu.SemaphoreType.DMA((9,))]
        + [pltpu.SemaphoreType.DMA((COPIES,))] * 2
        + [pltpu.SemaphoreType.DMA((sections,))] * 8
        + [pltpu.SemaphoreType.DMA((2,))] * 2
    )
    new_mom, search_in, search_out = pl.pallas_call(
        functools.partial(kernel, sections),
        out_shape=(
            jax.ShapeDtypeStruct((4, 128, 128), F32),
            jax.ShapeDtypeStruct((128, 128), BF16),
            jax.ShapeDtypeStruct((128, 128), BF16),
        ),
        in_specs=[hbm] * 7 + [smem] * 2,
        out_specs=(vmem, vmem, vmem),
        scratch_shapes=scratch,
        compiler_params=pltpu.CompilerParams(
            collective_id=0, has_side_effects=True, vmem_limit_bytes=60 * 1024 * 1024
        ),
        name="drain",
    )(
        saved_inputs.reshape(128, 4096), loss_grad.reshape(128, 4096), w_in[0], w_out[0],
        left_root[0, 0], right_root[0, 0], momentum[0, 0],
        jnp.swapaxes(owned_blocks, 1, 2), owned_count,
    )
    return new_mom[None, None], search_in[None], search_out[None]


def solution(mesh):
    placed = (
        P("section", None, "dp", None),
        P(None, "dp", None),
        P("section", None, None),
        P("section", None, None),
        P("section", "dp", None, None, None),
        P("section", "dp", None, None, None),
        P("section", "dp", None, None, None),
        P("section", None, None),
        P("section", None),
    )
    return jax.shard_map(
        functools.partial(on_device, mesh.shape["section"]),
        mesh=mesh,
        in_specs=placed,
        out_specs=(
            P("section", "dp", None, None, None),
            P("section", "dp", None),
            P("section", None, "dp"),
        ),
        check_vma=False,
    )
```

time: 136 us -> 125 us (0.919)
  local copies, waits for them, and re-layouts: 11 us -> 3.06 us
  Pallas kernels: 124 us -> 121 us
    unnamed x22 -> x7, local copies, waits for them, and re-layouts: 10.9 us -> 3.06 us
    pallas_call x1, Pallas kernels: 124 us -> 121 us  [on_device(): pl.pallas_call(functools.partial(kernel, sections), out_shape=(jax.ShapeD...]
where the time goes in v2:
time: 125 us; the launch traced here: 124 us
  Pallas kernels  121 us (97%)
  local copies, waits for them, and re-layouts  3.06 us (2%)
    pallas_call x1, Pallas kernels, on_device(): pl.pallas_call(functools.partial(kernel, sections), out_shape=(jax.ShapeD...  121 us
    unnamed x7, local copies, waits for them, and re-layouts  3.06 us

profile of v2, /device:TPU:1, one launch (start us, length us, event | category | flops | bytes accessed | tf_op | source)
XLA Modules:
  0.0 124.4 jit_solution(16455257085806633528)
XLA Ops:
  0.6 120.7 %drain.1 = (f32[4,128,128]{2,1,0:T(8,128)}, bf16[128,128]{1,0:T(8,128)(2,1)}, bf16[128,128]{1,0:T(8,128)(2,1)}) custom-call(bf16[128,4096]{1,0:T(8,128)(2,1)} %bitcast.11, bf16[128,4096]{1,0:T(8,128)(2,1)} %bitcast.12, bf16[4096,128]{1,0:T(8,128)(2,1)} %bitcast.13, bf16[128,4096]{1,0:T(8,128)(2,1)} %bitcast.14, bf16[4,128,128]{2,1,0:T(8,128)(2,1)} %bitcast.17, ...), custom_call_target="tpu_custom_call" | custom-call | tf_op jit(solution)/shard_map/drain/pallas_call | solution.py:755
  121.4 0.0 copy-start.1
  121.4 1.7 %copy.15 = f32[1,1,4,128,128]{4,3,2,1,0:T(8,128)} copy(f32[1,1,4,128,128]{4,3,2,1,0:T(8,128)} %bitcast.16) | data formatting | bytes 524288
  123.1 0.0 copy-done.1
  123.1 0.0 copy-start
  123.1 0.6 copy.16
  123.7 0.2 copy-done
  123.8 0.6 copy.17
Async XLA Ops:
  121.4 1.7 %copy-start.1 = (bf16[128,128]{1,0:T(8,128)(2,1)S(1)}, bf16[128,128]{1,0:T(8,128)(2,1)}, u32[]{:S(2)}) copy-start(bf16[128,128]{1,0:T(8,128)(2,1)} %get-tuple-element.7) | copy-start | bytes 98308
  123.1 0.8 copy-start

commit v3 on v2

--- a/solution.py
+++ b/solution.py
@@ -161,6 +161,12 @@
     def share_product(k):
         return to_section(m_o.at[places(k)], m_next.at[k], n_send.at[k], n_recv.at[k], below)
 
+    def pair_product(k):
+        return pltpu.make_async_remote_copy(
+            src_ref=m_next.at[k], dst_ref=m_next.at[k], send_sem=n_send.at[k], recv_sem=n_recv.at[k],
+            device_id={"dp": sibling}, device_id_type=MESH,
+        )
+
     pl.when(s > 1)(lambda: own_far().start())
     pl.when(s > 0)(lambda: own_near().start())
 
@@ -364,18 +370,6 @@
         product(odd)
         product(far)
 
-        @pl.when(wide & (n == 3))
-        def _():
-            m_sum.start(0, 0, 1)
-
-        @pl.when(wide & (n == 4))
-        def _():
-            m_sum.finish(0, 0, 1)
-            m_sum.start(1, 0, 1)
-
-        @pl.when(wide & (n == 5))
-        def _():
-            m_sum.finish(1, 0, 1)
         return carry
 
     steps = (last - s) // 2
@@ -386,16 +380,7 @@
         slice_near(last).wait_recv()
         product(last - s)
 
-    @pl.when(wide)
-    def _():
-        @pl.when(steps < 5)
-        def _():
-            m_sum.finish(0, 0, 1)
-            m_sum.start(1, 0, 1)
-
-        m_sum.start(0, 1, 1)
-        pl.when(steps < 6)(lambda: m_sum.finish(1, 0, 1))
-
+    pl.when(wide)(lambda: m_sum.start(0, 0, 2))
     pl.when((~wide) & (s < last))(lambda: m_sum.start(0, 0, 1))
 
     @pl.when(s <= EARLY)
@@ -405,8 +390,8 @@
 
     @pl.when(wide)
     def _():
-        m_sum.finish(0, 1, 1)
-        m_sum.start(1, 1, 1)
+        m_sum.finish(0, 0, 2)
+        m_sum.start(1, 0, 2)
 
     @pl.when(s <= EARLY)
     def _():
@@ -414,7 +399,7 @@
         roots_pack()
         outof.start(1)
 
-    pl.when(wide)(lambda: m_sum.finish(1, 1, 1))
+    pl.when(wide)(lambda: m_sum.finish(1, 0, 2))
 
     @pl.when((~wide) & (s < last))
     def _():
@@ -424,10 +409,10 @@
 
     @pl.when(~even)
     def _():
-        def give(k, carry):
-            share_product(k).start()
-            return carry
-        lax.fori_loop(0, last - s, give, 0)
+        def give(n, carry):
+            share_product(last - 1 - s - 2 * n - (1 - c)).start()
+            return carry
+        lax.fori_loop(0, (last - s) // 2, give, 0)
 
     pl.when(s > SOON)(lambda: go(roots_first()))
 
@@ -456,8 +441,7 @@
                 pass_far(low).start()
 
         def products(high, low):
-            share_product(high - s - 2).wait_recv()
-            share_product(low - s - 2).wait_recv()
+            share_product(high - s - 2 - c).wait_recv()
 
         def collect(n, carry):
             high, low = 15 - 2 * n, 14 - 2 * n
@@ -476,7 +460,14 @@
             acc[...] += own_term(high) + own_term(low)
             return carry
 
+        def spread(n, carry):
+            k = last - 2 - s - 2 * n - (1 - c)
+            share_product(k).wait_recv()
+            pair_product(k).start()
+            return carry
+
         lax.fori_loop(0, 7 - lowest, collect, 0)
+        lax.fori_loop(0, 8 - lowest, spread, 0)
         lax.fori_loop(0, 7 - lowest, add, 0)
 
         @pl.when(s < last - 1)
@@ -686,15 +677,21 @@
     def _():
         sent(share_state())
 
-        def given(k, carry):
-            share_product(k).wait_send()
-            return carry
-        lax.fori_loop(0, last - s, given, 0)
+        def given(n, carry):
+            share_product(last - 1 - s - 2 * n - (1 - c)).wait_send()
+            return carry
+        lax.fori_loop(0, (last - s) // 2, given, 0)
+
+    @pl.when(even)
+    def _():
+        def given_pair(n, carry):
+            pair_product(last - 2 - s - 2 * n - (1 - c)).wait_send()
+            return carry
+        lax.fori_loop(0, 8 - lowest, given_pair, 0)
 
     @pl.when(wide)
     def _():
-        m_sum.drain(0, 1)
-        m_sum.drain(1, 1)
+        m_sum.drain(0, 2)
         c_sum.drain(0, 2)
 
     @pl.when((~wide) & (s < last))

time: 125 us -> 122 us (0.976)
  Pallas kernels: 121 us -> 118 us
    pallas_call x1, Pallas kernels: 121 us -> 118 us  [on_device(): pl.pallas_call(functools.partial(kernel, sections), out_shape=(jax.ShapeD...]
where the time goes in v3:
time: 122 us
  Pallas kernels  118 us (97%)
  local copies, waits for them, and re-layouts  3.06 us (3%)
    pallas_call x1, Pallas kernels, on_device(): pl.pallas_call(functools.partial(kernel, sections), out_shape=(jax.ShapeD...  118 us
    unnamed x7, local copies, waits for them, and re-layouts  3.06 us

profile of v3, /device:TPU:1, one launch (start us, length us, event | category | flops | bytes accessed | tf_op | source)
XLA Modules:
  0.0 122.2 jit_solution(16197579848702238446)
XLA Ops:
  0.6 118.4 %drain.1 = (f32[4,128,128]{2,1,0:T(8,128)}, bf16[128,128]{1,0:T(8,128)(2,1)}, bf16[128,128]{1,0:T(8,128)(2,1)}) custom-call(bf16[128,4096]{1,0:T(8,128)(2,1)} %bitcast.11, bf16[128,4096]{1,0:T(8,128)(2,1)} %bitcast.12, bf16[4096,128]{1,0:T(8,128)(2,1)} %bitcast.13, bf16[128,4096]{1,0:T(8,128)(2,1)} %bitcast.14, bf16[4,128,128]{2,1,0:T(8,128)(2,1)} %bitcast.17, ...), custom_call_target="tpu_custom_call" | custom-call | tf_op jit(solution)/shard_map/drain/pallas_call | solution.py:752
  119.1 0.0 copy-start.1
  119.1 1.7 %copy.15 = f32[1,1,4,128,128]{4,3,2,1,0:T(8,128)} copy(f32[1,1,4,128,128]{4,3,2,1,0:T(8,128)} %bitcast.16) | data formatting | bytes 524288
  120.8 0.0 copy-done.1
  120.8 0.0 copy-start
  120.8 0.6 copy.16
  121.4 0.2 copy-done
  121.5 0.6 copy.17
Async XLA Ops:
  119.1 1.7 %copy-start.1 = (bf16[128,128]{1,0:T(8,128)(2,1)S(1)}, bf16[128,128]{1,0:T(8,128)(2,1)}, u32[]{:S(2)}) copy-start(bf16[128,128]{1,0:T(8,128)(2,1)} %get-tuple-element.7) | copy-start | bytes 98308
  120.8 0.8 copy-start

commit v4 on v3

--- a/solution.py
+++ b/solution.py
@@ -35,8 +35,8 @@
     newmom_ref, search_in_ref, search_out_ref,
     x_ref, gl_ref, win_ref, wout_ref, mom_ref,
     wz, pg, slope, base, acc, acc_out, act_t, slope_next, acc_next, m_next,
-    m_p, m_rc, m_o,
-    c_p, c_rc, c_o,
+    m_p, m_pc, m_q, m_rc, m_o,
+    c_p, c_pc, c_q, c_rc, c_o,
     i_p, i_rc, i_q, i_ra, i_t, i_rb,
     o_p, o_rc, o_q, o_ra, o_t, o_rb,
     r_x, r_pk, r_rk, r_sum, r_rc, r_home,
@@ -92,10 +92,11 @@
     barrier = pltpu.get_barrier_semaphore()
 
     def greet(i, carry):
-        pl.semaphore_signal(barrier, inc=1, device_id={"dp": lax.rem(dp + i, 32)}, device_id_type=MESH)
+        pl.semaphore_signal(barrier, inc=1, device_id={"dp": lax.rem(dp + 2 * i, 32)}, device_id_type=MESH)
         return carry
 
-    lax.fori_loop(1, 32, greet, 0)
+    lax.fori_loop(1, 16, greet, 0)
+    pl.semaphore_signal(barrier, inc=1, device_id={"dp": sibling}, device_id_type=MESH)
     below = lax.rem(s + last, sections)
     below_two = lax.rem(s + last - 1, sections)
     even = lax.rem(s, 2) == 0
@@ -119,7 +120,7 @@
         fetch(("left", h), left_hbm.at[:, rows], r_x.at[h, slots, 0])
         fetch(("right", h), right_hbm.at[:, rows], r_x.at[h, slots, 1])
 
-    pl.semaphore_wait(barrier, 35)
+    pl.semaphore_wait(barrier, 20)
 
     def to_section(source, target, send_sem, recv_sem, peer):
         return pltpu.make_async_remote_copy(
@@ -245,17 +246,31 @@
     c_p[...] = jnp.zeros_like(c_p)
 
     class Sum:
-        def __init__(self, name, p, rc, o):
-            self.name, self.p, self.rc, self.o = name, p, rc, o
+        def __init__(self, name, p, pc, q, rc, o):
+            self.name, self.p, self.pc, self.q, self.rc, self.o = name, p, pc, q, rc, o
+
+        def pair(self, stage, first, size):
+            part = pl.ds(first, size)
+            if stage == 0:
+                return [remote((self.name, "pair", 0), self.p.at[part, :, :, :, 1 - c], self.pc.at[part], sibling)]
+            mine = self.o.at[part, :, :, :, c]
+            return [remote((self.name, "pair", 1), mine, mine, sibling)]
 
         def start(self, stage, first, size):
             number = sid((self.name, stage, first))
             part = pl.ds(first, size)
+            if stage == 0:
+                go(self.pair(0, first, size))
+                land(self.pair(0, first, size))
+                for chunk in range(first, first + size):
+                    for h in range(2):
+                        both = self.p[chunk, h, :, :, c].astype(F32) + self.pc[chunk, h].astype(F32)
+                        self.q[chunk, h] = both.astype(BF16)
 
             def one(i, carry):
-                peer = lax.rem(dp + i, 32)
+                peer = lax.rem(dp + 2 * i, 32)
                 if stage == 0:
-                    source = self.p.at[part, :, peer // 8, lax.rem(peer // 2, 4), lax.rem(peer, 2)]
+                    source = self.q.at[part, :, peer // 8, lax.rem(peer // 2, 4)]
                     target = self.rc.at[i - 1, part]
                 else:
                     source = target = self.o.at[part, :, x, y, c]
@@ -265,7 +280,7 @@
                 ).start()
                 return carry
 
-            lax.fori_loop(1, 32, one, 0)
+            lax.fori_loop(1, 16, one, 0)
 
         def all_bytes(self, sems, stage, first, size):
             number = sid((self.name, stage, first))
@@ -276,14 +291,18 @@
             self.all_bytes(recv, stage, first, size)
             if stage == 0:
                 part = pl.ds(first, size)
-                total = self.p[part, :, x, y, c].astype(F32)
-                for i in range(31):
+                total = self.q[part, :, x, y].astype(F32)
+                for i in range(15):
                     total = total + self.rc[i, part].astype(F32)
                 self.o[part, :, x, y, c] = total.astype(BF16)
+            else:
+                go(self.pair(1, first, size))
+                land(self.pair(1, first, size))
 
         def drain(self, first, size):
             for stage in range(2):
                 self.all_bytes(send, stage, first, size)
+                sent(self.pair(stage, first, size))
 
     class Scatter:
         def __init__(self, name, p, rc, q, ra, t, rb):
@@ -346,8 +365,8 @@
             for stage in range(3):
                 sent(self.copies(stage))
 
-    m_sum = Sum("m", m_p, m_rc, m_o)
-    c_sum = Sum("c", c_p, c_rc, c_o)
+    m_sum = Sum("m", m_p, m_pc, m_q, m_rc, m_o)
+    c_sum = Sum("c", c_p, c_pc, c_q, c_rc, c_o)
     into = Scatter("i", i_p, i_rc, i_q, i_ra, i_t, i_rb)
     outof = Scatter("o", o_p, o_rc, o_q, o_ra, o_t, o_rb)
 
@@ -722,7 +741,7 @@
 
     def sum_room():
         return [
-            room(2, 2, 4, 4, 2, 16, 128), room(31, 2, 2, 16, 128), room(2, 2, 4, 4, 2, 16, 128),
+            room(2, 2, 4, 4, 2, 16, 128), room(2, 2, 4, 4, 16, 128), room(2, 2, 4, 4, 16, 128), room(15, 2, 2, 16, 128), room(2, 2, 4, 4, 2, 16, 128),
         ]
 
     def scatter_room():

time: 122 us -> 119 us (0.975)
  Pallas kernels: 118 us -> 115 us
    pallas_call x1, Pallas kernels: 118 us -> 115 us  [on_device(): pl.pallas_call(functools.partial(kernel, sections), out_shape=(jax.ShapeD...]
where the time goes in v4:
time: 119 us
  Pallas kernels  115 us (97%)
  local copies, waits for them, and re-layouts  3.06 us (3%)
    pallas_call x1, Pallas kernels, on_device(): pl.pallas_call(functools.partial(kernel, sections), out_shape=(jax.ShapeD...  115 us
    unnamed x7, local copies, waits for them, and re-layouts  3.06 us

profile of v4, /device:TPU:1, one launch (start us, length us, event | category | flops | bytes accessed | tf_op | source)
XLA Modules:
  0.0 118.5 jit_solution(7686414441344271577)
XLA Ops:
  0.6 114.8 %drain.1 = (f32[4,128,128]{2,1,0:T(8,128)}, bf16[128,128]{1,0:T(8,128)(2,1)}, bf16[128,128]{1,0:T(8,128)(2,1)}) custom-call(bf16[128,4096]{1,0:T(8,128)(2,1)} %bitcast.11, bf16[128,4096]{1,0:T(8,128)(2,1)} %bitcast.12, bf16[4096,128]{1,0:T(8,128)(2,1)} %bitcast.13, bf16[128,4096]{1,0:T(8,128)(2,1)} %bitcast.14, bf16[4,128,128]{2,1,0:T(8,128)(2,1)} %bitcast.17, ...), custom_call_target="tpu_custom_call" | custom-call | tf_op jit(solution)/shard_map/drain/pallas_call | solution.py:771
  115.4 0.0 copy-start.1
  115.4 1.7 %copy.15 = f32[1,1,4,128,128]{4,3,2,1,0:T(8,128)} copy(f32[1,1,4,128,128]{4,3,2,1,0:T(8,128)} %bitcast.16) | data formatting | bytes 524288
  117.1 0.0 copy-done.1
  117.1 0.0 copy-start
  117.1 0.6 copy.16
  117.7 0.2 copy-done
  117.9 0.6 copy.17
Async XLA Ops:
  115.4 1.7 %copy-start.1 = (bf16[128,128]{1,0:T(8,128)(2,1)S(1)}, bf16[128,128]{1,0:T(8,128)(2,1)}, u32[]{:S(2)}) copy-start(bf16[128,128]{1,0:T(8,128)(2,1)} %get-tuple-element.7) | copy-start | bytes 98308
  117.1 0.8 copy-start

commit v5 on v4

--- a/solution.py
+++ b/solution.py
@@ -260,7 +260,6 @@
             number = sid((self.name, stage, first))
             part = pl.ds(first, size)
             if stage == 0:
-                go(self.pair(0, first, size))
                 land(self.pair(0, first, size))
                 for chunk in range(first, first + size):
                     for h in range(2):
@@ -399,6 +398,8 @@
         slice_near(last).wait_recv()
         product(last - s)
 
+    pl.when(wide)(lambda: go(m_sum.pair(0, 0, 2)))
+    pl.when((~wide) & (s < last))(lambda: go(m_sum.pair(0, 0, 1)))
     pl.when(wide)(lambda: m_sum.start(0, 0, 2))
     pl.when((~wide) & (s < last))(lambda: m_sum.start(0, 0, 1))
 
@@ -532,11 +533,13 @@
 
     lax.fori_loop(0, (last - s) // 2, cross_two, 0)
     pl.when(even)(lambda: cross(last))
+    pl.when(wide)(lambda: go(c_sum.pair(0, 0, 2)))
+    pl.when((~wide) & (s < last))(lambda: go(c_sum.pair(0, 0, 1)))
+
+    into.fill(pg[s].astype(F32).T.astype(BF16), x_ref)
+    into.start(0)
     pl.when(wide)(lambda: c_sum.start(0, 0, 2))
     pl.when((~wide) & (s < last))(lambda: c_sum.start(0, 0, 1))
-
-    into.fill(pg[s].astype(F32).T.astype(BF16), x_ref)
-    into.start(0)
 
     into.finish(0)
     into.start(1)

time: 119 us -> 119 us (level)
  no operation moved by 1% of the time
where the time goes in v5:
time: 119 us
  Pallas kernels  115 us (97%)
  local copies, waits for them, and re-layouts  3.06 us (3%)
    pallas_call x1, Pallas kernels, on_device(): pl.pallas_call(functools.partial(kernel, sections), out_shape=(jax.ShapeD...  115 us
    unnamed x7, local copies, waits for them, and re-layouts  3.06 us

profile of v5, /device:TPU:1, one launch (start us, length us, event | category | flops | bytes accessed | tf_op | source)
XLA Modules:
  0.0 118.6 jit_solution(9870704962404014307)
XLA Ops:
  0.6 114.9 %drain.1 = (f32[4,128,128]{2,1,0:T(8,128)}, bf16[128,128]{1,0:T(8,128)(2,1)}, bf16[128,128]{1,0:T(8,128)(2,1)}) custom-call(bf16[128,4096]{1,0:T(8,128)(2,1)} %bitcast.11, bf16[128,4096]{1,0:T(8,128)(2,1)} %bitcast.12, bf16[4096,128]{1,0:T(8,128)(2,1)} %bitcast.13, bf16[128,4096]{1,0:T(8,128)(2,1)} %bitcast.14, bf16[4,128,128]{2,1,0:T(8,128)(2,1)} %bitcast.17, ...), custom_call_target="tpu_custom_call" | custom-call | tf_op jit(solution)/shard_map/drain/pallas_call | solution.py:774
  115.6 0.0 copy-start.1
  115.6 1.7 %copy.15 = f32[1,1,4,128,128]{4,3,2,1,0:T(8,128)} copy(f32[1,1,4,128,128]{4,3,2,1,0:T(8,128)} %bitcast.16) | data formatting | bytes 524288
  117.3 0.0 copy-done.1
  117.3 0.0 copy-start
  117.3 0.6 copy.16
  117.9 0.2 copy-done
  118.0 0.6 copy.17
Async XLA Ops:
  115.6 1.7 %copy-start.1 = (bf16[128,128]{1,0:T(8,128)(2,1)S(1)}, bf16[128,128]{1,0:T(8,128)(2,1)}, u32[]{:S(2)}) copy-start(bf16[128,128]{1,0:T(8,128)(2,1)} %get-tuple-element.7) | copy-start | bytes 98308
  117.3 0.8 copy-start
